TPU v7x, 32 devices: a whole 2x2x4 slice. The times are simulated.
32 devices in a mesh: row: 4 (over y, core), col: 8 (over z, x).
Axes of the slice: x: 2, y: 2, z: 4, core: 2. Of those that a mesh axis runs over, the one named last changes fastest.
Arguments:
- fringes: bfloat16 [32768, 32768], P(('row', 'col')), may hold values from -24 to 24
- lobe_bounds: int32 [64, 2], replicated, may hold values from 0 to 4096, as said below
- zone_index: int32 [1024, 64], P(('row', 'col')), may hold values from 0 to 1023
- zone_table: float32 [4, 1024], P(None, ('row', 'col')), may hold values from -6 to 6
Outputs:
- heights: bfloat16 [16384, 32768], P(('row', 'col'))
Inputs may be any that keep to these rules, and one draw needn't show every extreme that they name: For every band t, lobe_bounds[t, 0] < lobe_bounds[t, 1]; some band starts at 0 and some band ends at 4096.
All inputs are finite; a program needn't handle non-finite values.
Results may differ from a plain program's by a relative error of at most 0.023.
Values may be sent and summed in bfloat16 or wider, within the bound.
No kernel may reach another device: no remote copies, remote signals or barrier semaphores. Data moves between devices by JAX's collectives and lax.ppermute only.
A program may use at most 192 MiB of HBM per device.

v0:
```python
import math

import jax
import jax.numpy as jnp
from jax import lax
from jax.sharding import PartitionSpec as P

W = 32768
H = 32768
W1 = 128
H1 = 128
KY_TILES = 64
ZB_R = 16
ZB_C = 512
LOBE = 4096
LOBE_START = 4096


damping_floor = 0.5


def phase_pair(first_count, second_count, period, offset):
    first_index = jnp.arange(first_count, dtype=jnp.int32)[:, None]
    second_index = jnp.arange(second_count, dtype=jnp.int32)[None, :] + offset
    turn_count = first_index * second_index % period
    angles = turn_count.astype(jnp.float32) * (2.0 * math.pi / period)
    return (jnp.cos(angles), jnp.sin(angles))


def table_pair(first_count, second_count, period, offset):
    cosine, sine_part = phase_pair(first_count, second_count, period, offset)
    return (cosine.astype(jnp.bfloat16), sine_part.astype(jnp.bfloat16))


def complex_mix(pattern, real_part, imag_part, cosine, sine_part, direction):
    real_cos = jnp.einsum(pattern, real_part, cosine, preferred_element_type=jnp.float32)
    imag_sin = jnp.einsum(pattern, imag_part, sine_part, preferred_element_type=jnp.float32)
    imag_cos = jnp.einsum(pattern, imag_part, cosine, preferred_element_type=jnp.float32)
    real_sin = jnp.einsum(pattern, real_part, sine_part, preferred_element_type=jnp.float32)
    return (real_cos - direction * imag_sin, imag_cos + direction * real_sin)


def apply_twist(real_part, imag_part, cosine, sine_part, direction):
    out_real = real_part * cosine - direction * (imag_part * sine_part)
    out_imag = imag_part * cosine + direction * (real_part * sine_part)
    return (out_real, out_imag)


def row_forward(rows_block):
    row_total = rows_block.shape[0]
    shaped = rows_block.reshape(row_total, W1, W // W1)
    cosine, sine_part = table_pair(W1, W1, W1, 0)
    first_real = jnp.einsum("rab,ak->rkb", shaped, cosine, preferred_element_type=jnp.float32)
    first_imag = -jnp.einsum("rab,ak->rkb", shaped, sine_part, preferred_element_type=jnp.float32)
    twist_real, twist_imag = phase_pair(W1, W // W1, W, 0)
    middle_real, middle_imag = apply_twist(first_real, first_imag, twist_real, twist_imag, -1.0)
    middle_real = middle_real.astype(jnp.bfloat16)
    middle_imag = middle_imag.astype(jnp.bfloat16)
    cosine, sine_part = table_pair(W // W1, LOBE // W1, W // W1, LOBE_START // W1)
    lobe_real, lobe_imag = complex_mix(
        "rkb,bj->jkr", middle_real, middle_imag, cosine, sine_part, -1.0
    )
    return jnp.stack([lobe_real, lobe_imag]).reshape(2, LOBE, row_total).astype(jnp.bfloat16)


def column_pass(columns, column_index, lower_edge, upper_edge):
    col_total = columns.shape[1]
    second_len = H // H1
    shaped_real = columns[0].reshape(col_total, H1, second_len)
    shaped_imag = columns[1].reshape(col_total, H1, second_len)
    cosine, sine_part = table_pair(H1, H1, H1, 0)
    first_real, first_imag = complex_mix(
        "cab,ak->ckb", shaped_real, shaped_imag, cosine, sine_part, -1.0
    )
    twist_real, twist_imag = phase_pair(H1, second_len, H, 0)
    middle_real, middle_imag = apply_twist(first_real, first_imag, twist_real, twist_imag, -1.0)
    middle_real = middle_real.astype(jnp.bfloat16)
    middle_imag = middle_imag.astype(jnp.bfloat16)
    cosine, sine_part = table_pair(second_len, second_len, second_len, 0)
    spectrum_real, spectrum_imag = complex_mix(
        "ckb,bm->cmk", middle_real, middle_imag, cosine, sine_part, -1.0
    )
    spectrum_real = spectrum_real.reshape(col_total, H)
    spectrum_imag = spectrum_imag.reshape(col_total, H)
    lower_rows = jnp.repeat(lower_edge, H // KY_TILES)
    upper_rows = jnp.repeat(upper_edge, H // KY_TILES)
    keep_mask = (column_index[:, None] >= lower_rows[None, :]) & (
        column_index[:, None] < upper_rows[None, :]
    )
    masked_real = jnp.where(keep_mask, spectrum_real, 0.0)
    masked_imag = jnp.where(keep_mask, spectrum_imag, 0.0)
    half_rows = H // 2
    fold_scale = 1.0 / (H * W)
    folded_real = ((masked_real[:, :half_rows] + masked_real[:, half_rows:]) * fold_scale).astype(
        jnp.bfloat16
    )
    folded_imag = ((masked_imag[:, :half_rows] + masked_imag[:, half_rows:]) * fold_scale).astype(
        jnp.bfloat16
    )
    fold_len = second_len // 2
    folded_real = folded_real.reshape(col_total, fold_len, H1)
    folded_imag = folded_imag.reshape(col_total, fold_len, H1)
    cosine, sine_part = table_pair(fold_len, fold_len, fold_len, 0)
    half_real, half_imag = complex_mix(
        "cmk,mq->cqk", folded_real, folded_imag, cosine, sine_part, 1.0
    )
    twist_real, twist_imag = phase_pair(fold_len, H1, half_rows, 0)
    middle_real, middle_imag = apply_twist(half_real, half_imag, twist_real, twist_imag, 1.0)
    middle_real = middle_real.astype(jnp.bfloat16)
    middle_imag = middle_imag.astype(jnp.bfloat16)
    cosine, sine_part = table_pair(H1, H1, H1, 0)
    out_real, out_imag = complex_mix(
        "cqk,kp->cpq", middle_real, middle_imag, cosine, sine_part, 1.0
    )
    return jnp.stack([out_real, out_imag]).reshape(2, col_total, half_rows).astype(jnp.bfloat16)


def height_map(field_real, field_imag, coefficients):
    magnitude = jnp.sqrt(field_real * field_real + field_imag * field_imag)
    sine_value = field_imag / jnp.maximum(magnitude, damping_floor)
    row_total = field_real.shape[0]
    sine_value = sine_value.reshape(row_total // ZB_R, ZB_R, W // ZB_C, ZB_C)
    expanded = coefficients[:, :, None, :, None]
    heights = expanded[0] + sine_value * (
        expanded[1] + sine_value * (expanded[2] + sine_value * expanded[3])
    )
    return heights.reshape(row_total, W).astype(jnp.bfloat16)


def row_inverse(segment, coefficients):
    row_total = segment.shape[2]
    shaped_real = segment[0].reshape(LOBE // W1, W1, row_total)
    shaped_imag = segment[1].reshape(LOBE // W1, W1, row_total)
    cosine, sine_part = table_pair(LOBE // W1, W // W1, W // W1, 0)
    pixel_real, pixel_imag = complex_mix(
        "jkr,jq->rkq", shaped_real, shaped_imag, cosine, sine_part, 1.0
    )
    twist_real, twist_imag = phase_pair(W1, W // W1, W, 0)
    middle_real, middle_imag = apply_twist(pixel_real, pixel_imag, twist_real, twist_imag, 1.0)
    middle_real = middle_real.astype(jnp.bfloat16)
    middle_imag = middle_imag.astype(jnp.bfloat16)
    cosine, sine_part = table_pair(W1, W1, W1, 0)
    field_real, field_imag = complex_mix(
        "rkq,kp->rpq", middle_real, middle_imag, cosine, sine_part, 1.0
    )
    return height_map(
        field_real.reshape(row_total, W), field_imag.reshape(row_total, W), coefficients
    )


def body(fringes, lobe_bounds, zone_index, zone_table):
    row_count = fringes.shape[0]
    row_block = math.gcd(row_count, 64)

    def fill_block(block_number, buffer):
        row_start = block_number * row_block
        rows_block = lax.dynamic_slice_in_dim(fringes, row_start, row_block, 0)
        return lax.dynamic_update_slice_in_dim(buffer, row_forward(rows_block), row_start, 2)

    stacked = lax.fori_loop(
        0, row_count // row_block, fill_block, jnp.zeros((2, LOBE, row_count), jnp.bfloat16)
    )
    row_size = lax.axis_size("row")
    col_size = lax.axis_size("col")
    local_cols = LOBE // (row_size * col_size)
    columns = lax.all_to_all(stacked, ("row", "col"), split_axis=1, concat_axis=2, tiled=True)
    column_index = lax.axis_index(("row", "col")) * local_cols + jnp.arange(
        local_cols, dtype=jnp.int32
    )
    field_cols = column_pass(columns, column_index, lobe_bounds[:, 0], lobe_bounds[:, 1])
    out_count = field_cols.shape[2] // (row_size * col_size)
    field_rows = lax.all_to_all(field_cols, ("row", "col"), split_axis=2, concat_axis=1, tiled=True)
    full_table = lax.all_gather(zone_table, ("row", "col"), axis=1, tiled=True)
    zone_count = full_table.shape[1]
    flat_zones = zone_index.reshape(-1)
    onehot = (jnp.arange(zone_count, dtype=jnp.int32)[:, None] == flat_zones[None, :]).astype(
        jnp.float32
    )
    coefficients = jnp.dot(
        full_table, onehot, precision=lax.Precision.HIGHEST, preferred_element_type=jnp.float32
    )
    coefficients = coefficients.reshape(4, zone_index.shape[0], zone_index.shape[1])

    def height_block(block_number, buffer):
        row_start = block_number * ZB_R
        segment = lax.dynamic_slice_in_dim(field_rows, row_start, ZB_R, 2)
        block_coefficients = lax.dynamic_slice_in_dim(coefficients, block_number, 1, 1)
        return lax.dynamic_update_slice_in_dim(
            buffer, row_inverse(segment, block_coefficients), row_start, 0
        )

    return lax.fori_loop(
        0, out_count // ZB_R, height_block, jnp.zeros((out_count, W), jnp.bfloat16)
    )


def solution(mesh):
    placed = (P(("row", "col"), None), P(), P(("row", "col"), None), P(None, ("row", "col")))
    return jax.shard_map(
        body, mesh=mesh, in_specs=placed, out_specs=P(("row", "col"), None), check_vma=False
    )
```

profile of v0, /device:TPU:0, one launch (start us, length us, event | category | flops | bytes accessed | tf_op | source)
XLA Modules:
  0.0 1685.0 jit_solution(17695644761754359935)
XLA Ops:
  6.1 265.0 %while.32 = (s32[]{:T(128)}, bf16[2,4096,1024]{1,2,0:T(8,128)(2,1)}, bf16[1024,32768]{1,0:T(8,128)(2,1)}, s32[]{:T(128)}, s32[]{:T(128)}, /*index=5*/s32[]{:T(128)}, s32[]{:T(128)}) while((s32[]{:T(128)}, bf16[2,4096,1024]{1,2,0:T(8,128)(2,1)}, bf16[1024,32768]{1,0:T(8,128)(2,1)}, s32[]{:T(128)}, s32[]{:T(128)}, /*index=5*/s32[]{:T(128)}, ...), condition=%wide.region_1.2_spmd, body=%wide.region_0.1_spmd.sunk | while | flops 1638793216 | bytes 77071104 | solution.py:160
  271.1 41.6 %copy.27 = bf16[2,4096,1024]{2,0,1:T(2,128)(2,1)} copy(bf16[2,4096,1024]{1,2,0:T(8,128)(2,1)} %get-tuple-element.249) | data formatting | bytes 33554432 | tf_op jit(solution)/shard_map/while | solution.py:160
  323.1 366.5 %all-to-all-done = bf16[2,4096,1024]{2,0,1:T(2,128)(2,1)} async-done(((bf16[2,4096,1024]{2,0,1:T(2,128)(2,1)}), bf16[2,4096,1024]{2,0,1:T(2,128)(2,1)}, u32[]{:S(2)}, u32[]{:S(2)}) %all-to-all-start) | async-done | bytes 16777248 | tf_op jit(solution)/shard_map/all_to_all | solution.py:166
  689.6 15.7 copy.56
  711.7 13.9 reshape_squeeze.7
  725.6 14.0 reshape_squeeze.6
  739.6 11.8 fusion.211
  751.4 8.7 fusion.209
  760.1 11.0 multiply_add_fusion.1
  771.1 19.4 %fusion.141 = (bf16[128,128,256]{2,1,0:T(8,128)(2,1)S(1)}, bf16[128,128,256]{2,1,0:T(8,128)(2,1)}) fusion(f32[128,128,256]{2,0,1:T(8,128)} %multiply_add_fusion.1, f32[128,256]{1,0:T(8,128)S(1)} %get-tuple-element.293, f32[128,256]{1,0:T(8,128)S(1)} %get-tuple-element.294, f32[128,128,256]{2,0,1:T(8,128)} %fusion.211, ...), kind=kOutput, calls=%fused_computation.189 | convolution fusion | flops 1124319232 | bytes 58982400 | tf_op jit(solution)/shard_map/cab,ak->ckb/dot_general | solution.py:37
  799.2 12.9 fusion.171
  812.1 15.6 multiply_subtract_fusion
  827.7 15.5 multiply_add_fusion
  843.2 40.1 %bitcast_select_fusion.1 = (f32[128,32768]{1,0:T(8,128)S(1)}, f32[128,32768]{1,0:T(8,128)}) fusion(f32[16,8,256,128]{3,2,1,0:T(8,128)} %bitcast.326, s32[32768]{0:T(1024)S(1)} %bitcast.343, s32[32768]{0:T(1024)S(1)} %bitcast.344, s32[128]{0:T(128)S(1)} %iota_add_fusion.1, f32[16,8,256,128]{3,2,1,0:T(8,128)} %bitcast.327), kind=kLoop, calls=%fused_computation.180 | loop fusion | flops 20971520 | bytes 67371520 | tf_op jit(solution)/shard_map/jit(_where)/select_n | solution.py:90
  907.6 10.3 fusion.148
  935.2 17.7 %copy.31 = bf16[1,128,16384]{1,0,2:T(2,128)(2,1)} copy(bf16[1,128,16384]{2,1,0:T(8,128)(2,1)} %stack.24) | data formatting | bytes 8388608 | tf_op jit(solution)/shard_map/stack | solution.py:115
  968.3 17.7 %copy.32 = bf16[1,128,16384]{1,0,2:T(2,128)(2,1)} copy(bf16[1,128,16384]{2,1,0:T(8,128)(2,1)} %stack.25) | data formatting | bytes 8388608 | tf_op jit(solution)/shard_map/stack | solution.py:115
  986.0 19.7 %pad_maximum_fusion = bf16[2,128,16384]{1,0,2:T(2,128)(2,1)} fusion(bf16[1,128,16384]{1,0,2:T(2,128)(2,1)} %copy.32, bf16[1,128,16384]{1,0,2:T(2,128)(2,1)} %copy.31), kind=kLoop, calls=%fused_computation.197 | loop fusion | flops 16777216 | bytes 16777216 | tf_op jit(solution)/shard_map/stack | solution.py:115
  1005.8 15.8 all-to-all-start.1
  1021.6 242.5 %all-gather = f32[32,32,4]{1,2,0:T(4,128)S(1)} all-gather(f32[1,32,4]{1,2,0:T(4,128)S(1)} %bitcast.345), channel_id=1, replica_groups=mesh['row'=4,'col'=8] {'row','col'}, dimensions={0}, use_global_device_ids=true | all-gather | bytes 16896 | tf_op jit(solution)/shard_map/all_gather | solution.py:173
  1267.0 12.2 copy.33
  1279.2 13.6 all_to_all.30
  1292.8 11.0 broadcast_in_dim.51
  1303.8 380.8 %while.33 = (s32[]{:T(128)}, bf16[512,32768]{1,0:T(8,128)(2,1)}, f32[4,32,64]{2,1,0:T(8,128)S(1)}, bf16[2,4096,512]{1,2,0:T(8,128)(2,1)}, s32[]{:T(128)}, /*inde...) while((s32[]{:T(128)}, bf16[512,32768]{1,0:T(8,128)(2,1)}, f32[4,32,64]{2,1,0:T(8,128)S(1)}, ...), condition=%wide.region_3.4_spmd, body=%wide.region_2.3_spmd.sunk | while | flops 685604864 | bytes 49286372 | solution.py:192
  (966 shorter events, 732.5 us)
Async XLA Ops:
  312.8 9.6 copy-start.7
  312.8 376.8 %all-to-all-start = ((bf16[2,4096,1024]{2,0,1:T(2,128)(2,1)}), bf16[2,4096,1024]{2,0,1:T(2,128)(2,1)}, u32[]{:S(2)}, u32[]{:S(2)}) async-start(bf16[2,4096,1024]{2,0,1:T(2,128)(2,1)} %copy.27), calls=%async_computation | async-start | bytes 33554432 | tf_op jit(solution)/shard_map/all_to_all | solution.py:166
  739.6 11.8 copy-start.1
  739.6 20.5 %slice-start = ((s8[8388608]{0:T(1024)(128)(4,1)}), s8[4194304]{0:T(1024)(128)(4,1)S(1)}, s32[]{:S(2)}) async-start(s8[8388608]{0:T(1024)(128)(4,1)} %bitcast.328), calls=%async_computation.2 | async-start | bytes 8388608
  751.4 8.7 slice-start.1
  790.5 8.7 copy-start
  902.8 4.7 copy-start.3
  902.8 4.7 copy-start.4
  917.9 6.3 copy-start.2
  1005.8 15.8 copy-start.5
  1005.8 15.9 copy-start.6
  1005.8 261.2 %all-to-all-start.1 = ((bf16[2,128,16384]{1,0,2:T(2,128)(2,1)}), bf16[2,128,16384]{1,0,2:T(2,128)(2,1)}, u32[]{:S(2)}, u32[]{:S(2)}) async-start(bf16[2,128,16384]{1,0,2:T(2,128)(2,1)} %pad_maximum_fusion), calls=%async_computation.1 | async-start | bytes 16777216 | tf_op jit(solution)/shard_map/all_to_all | solution.py:172
where the time goes:
time: 1700 us; the launch traced here: 1690 us
  matrix products  490 us (29%)
  local copies, waits for them, and re-layouts  375 us (22%)
  waiting for transfers between devices  366 us (22%)
  blocking collectives  243 us (14%)
  other arithmetic  182 us (11%)
  starting transfers between devices  23.4 us (1%)
    all_to_all x1, waiting for transfers between devices, body(): lax.all_to_all(stacked, ('row', 'col'), split_axis=1, concat_axis=2, tile...  366 us
    all_gather x1, blocking collectives, body(): full_table = lax.all_gather(zone_table, ('row', 'col'), axis=1, tiled=True)  243 us
    while x368, local copies, waits for them, and re-layouts  139 us
    dot_general x84, matrix products, complex_mix(): jnp.einsum(pattern, imag_part, sine_part, preferred_element_type=jnp.floa...  118 us
    dot_general x84, matrix products, complex_mix(): jnp.einsum(pattern, real_part, sine_part, preferred_element_type=jnp.floa...  99.7 us
    dot_general x84, matrix products, complex_mix(): jnp.einsum(pattern, real_part, cosine, preferred_element_type=jnp.float32)  92.6 us
    dot_general x84, matrix products, complex_mix(): jnp.einsum(pattern, imag_part, cosine, preferred_element_type=jnp.float32)  91.9 us
    dynamic_update_slice x32, other arithmetic, height_block(): lax.dynamic_update_slice_in_dim(buffer, row_inverse(segment, block_coeffi...  71.6 us
  transfers between devices with their start and end apart: 2, of which 1 were waited for; matrix products, arithmetic and copies ran while one was open for 0% of the time, Pallas kernels for 0%

commit v1 on v0

v1 whole, which is shorter than its diff:
```python
import functools
import math

import jax
import jax.numpy as jnp
import ml_dtypes
import numpy as np
from jax import lax
from jax.experimental import pallas as pl
from jax.experimental.pallas import tpu as pltpu
from jax.sharding import Mesh
from jax.sharding import PartitionSpec as P

ZB_R = 16
LOBE = 4096
LOBE_START = 4096
DAMPING_FLOOR = 0.5

RADIX = 64
UNITS = RADIX // 2
GROUP = 16
HALVES = UNITS // GROUP
LANES = 128
ROW_PARTS = 4

f32 = jnp.float32
bf16 = jnp.bfloat16
VMEM_LIMIT = 58 * 1024 * 1024


def plus(x, y):
    if x is None:
        return y
    if y is None:
        return x
    return (x[0] + y[0], x[1] + y[1])


def minus(x, y):
    if y is None:
        return x
    if x is None:
        return (-y[0], -y[1])
    return (x[0] - y[0], x[1] - y[1])


def plus_i(x, y, sign):
    if y is None:
        return x
    if x is None:
        return (-y[1], y[0]) if sign > 0 else (y[1], -y[0])
    if sign > 0:
        return (x[0] - y[1], x[1] + y[0])
    return (x[0] + y[1], x[1] - y[0])


def turn(x, num, den):
    num %= den
    if x is None or num == 0:
        return x
    re, im = x
    if 4 * num == den:
        return (-im, re)
    if 2 * num == den:
        return (-re, -im)
    if 4 * num == 3 * den:
        return (im, -re)
    half = math.sqrt(0.5)
    if 8 * num == den:
        return ((re - im) * half, (re + im) * half)
    if 8 * num == 3 * den:
        return ((re + im) * -half, (re - im) * half)
    if 8 * num == 5 * den:
        return ((im - re) * half, (re + im) * -half)
    if 8 * num == 7 * den:
        return ((re + im) * half, (im - re) * half)
    c = math.cos(2 * math.pi * num / den)
    s = math.sin(2 * math.pi * num / den)
    return (re * c - im * s, im * c + re * s)


def complex_fft(xs, sign):
    n = len(xs)
    if n == 1:
        return list(xs)
    if n == 2:
        return [plus(xs[0], xs[1]), minus(xs[0], xs[1])]
    even = complex_fft(xs[0::2], sign)
    one = complex_fft(xs[1::4], sign)
    three = complex_fft(xs[3::4], sign)
    out = [None] * n
    for k in range(n // 4):
        t1 = turn(one[k], sign * k, n)
        t3 = turn(three[k], sign * 3 * k, n)
        total, diff = plus(t1, t3), minus(t1, t3)
        out[k] = plus(even[k], total)
        out[k + n // 2] = minus(even[k], total)
        out[k + n // 4] = plus_i(even[k + n // 4], diff, sign)
        out[k + 3 * n // 4] = plus_i(even[k + n // 4], diff, -sign)
    return out


def real_fft(xs):
    n = len(xs)
    if n == 1:
        return [(xs[0], None)]
    if n == 2:
        return [(xs[0] + xs[1], None), (xs[0] - xs[1], None)]
    even = real_fft(xs[0::2])
    one = real_fft(xs[1::4])
    three = real_fft(xs[3::4])
    out = [None] * (n // 2 + 1)
    total, diff = one[0][0] + three[0][0], one[0][0] - three[0][0]
    out[0] = (even[0][0] + total, None)
    out[n // 2] = (even[0][0] - total, None)
    out[n // 4] = (even[n // 4][0], -diff)
    for k in range(1, n // 8 + 1):
        if one[k][1] is None:
            c1, s1 = math.cos(2 * math.pi * k / n), math.sin(2 * math.pi * k / n)
            c3, s3 = math.cos(6 * math.pi * k / n), math.sin(6 * math.pi * k / n)
            t1 = (one[k][0] * c1, one[k][0] * -s1)
            t3 = (three[k][0] * c3, three[k][0] * -s3)
        else:
            t1 = turn(one[k], -k, n)
            t3 = turn(three[k], -3 * k, n)
        total, diff = plus(t1, t3), minus(t1, t3)
        low, high = even[k], even[n // 4 - k]
        if low[1] is None:
            out[k] = (low[0] + total[0], total[1])
            out[n // 2 - k] = (low[0] - total[0], total[1])
        else:
            out[k] = (low[0] + total[0], low[1] + total[1])
            out[n // 2 - k] = (low[0] - total[0], total[1] - low[1])
        if k != n // 4 - k:
            if high[1] is None:
                out[n // 4 + k] = (high[0] + diff[1], -diff[0])
                out[n // 4 - k] = (high[0] - diff[1], -diff[0])
            else:
                out[n // 4 + k] = (high[0] + diff[1], -(high[1] + diff[0]))
                out[n // 4 - k] = (high[0] - diff[1], high[1] - diff[0])
    return out


def cos_sin(turns, period):
    angles = (turns % period) * (2.0 * np.pi / period)
    return np.cos(angles), np.sin(angles)


def as_bf16(table):
    return table.astype(np.float32).astype(ml_dtypes.bfloat16)


def forward_tables(width):
    points = width // RADIX
    per_residue = LOBE // RADIX
    b = np.arange(points)[:, None]
    twist_cos, twist_sin = cos_sin(np.arange(UNITS)[:, None] * b.T, width)
    j = LOBE_START // RADIX + np.arange(per_residue)[None, :]
    c1, s1 = cos_sin(b * j, points)
    c2, s2 = cos_sin(b * (j + 1), points)
    mix = np.block([[c1, c2, -s1, -s2], [s1, -s2, c1, -c2]])
    c3, s3 = cos_sin(b * (2 * j + 1), 2 * points)
    zero = np.zeros_like(c1)
    mix_real = np.block([[c1, zero, -s1, zero], [zero, c3, zero, -s3]])
    return twist_cos.astype(np.float32), twist_sin.astype(np.float32), as_bf16(mix), as_bf16(mix_real)


def inverse_tables(width):
    points = width // RADIX
    per_residue = LOBE // RADIX
    q = np.arange(points)[None, :]
    twist_cos, twist_sin = cos_sin(np.arange(RADIX)[:, None] * q, width)
    c, s = cos_sin(np.arange(per_residue)[:, None] * q, points)
    zero = np.zeros_like(c)
    mix = np.block([[c, s, zero, zero], [zero, zero, c, s], [-s, c, zero, zero], [zero, zero, -s, c]])
    return twist_cos.astype(np.float32), twist_sin.astype(np.float32), as_bf16(mix)


def column_tables(rows):
    part = rows // ROW_PARTS
    b = np.arange(part)[None, :]
    m = np.arange(part)[:, None]
    forward = []
    for q in range(ROW_PARTS):
        c, s = cos_sin(b * (q + ROW_PARTS * m), rows)
        forward.append(np.concatenate([c, s], axis=1))
    out_row = np.arange(rows // 2)[:, None]
    order = (np.arange(ROW_PARTS)[:, None] + ROW_PARTS * np.arange(part // 2)[None, :]).reshape(1, -1)
    c, s = cos_sin(out_row * order, rows // 2)
    return as_bf16(np.stack(forward)), as_bf16(np.concatenate([c, s], axis=1))


def unit_columns(unit):
    lane = jnp.arange(LANES, dtype=jnp.int32)
    per_residue = LOBE // RADIX
    second = jnp.where(unit == 0, RADIX // 2, RADIX - unit)
    return RADIX * (lane % per_residue) + jnp.where(lane < per_residue, unit, second)


def launch(kernel, held, operands, in_specs, aliases=None, **options):
    count = len(held)
    return pl.pallas_call(
        lambda *refs: kernel(*refs[count:]),
        in_specs=[pl.BlockSpec(memory_space=pl.ANY)] * count + in_specs,
        input_output_aliases={count + k: v for k, v in (aliases or {}).items()},
        compiler_params=pltpu.CompilerParams(vmem_limit_bytes=VMEM_LIMIT),
        cost_estimate=pl.CostEstimate(flops=1, bytes_accessed=1, transcendentals=0),
        **options,
    )(*held, *operands)


def whole(array):
    return pl.BlockSpec(array.shape, lambda *_: (0,) * array.ndim)


def forward_kernel(x_ref, cos_ref, sin_ref, mix_ref, real_ref, *refs):
    outs, z_ref = refs[:HALVES], refs[HALVES]
    rows, width = x_ref.shape
    points = width // RADIX
    tiles = points // LANES

    def tile(i, carry):
        r = pl.multiple_of((i // tiles) * 16, 16)
        l = pl.multiple_of((i % tiles) * LANES, LANES)
        here = pl.ds(r, 16)
        xs = [x_ref[here, pl.ds(a * points + l, LANES)].astype(f32) for a in range(RADIX)]
        spectrum = real_fft(xs)
        z_ref[0, here, pl.ds(l, LANES)] = spectrum[0][0].astype(bf16)
        z_ref[0, here, pl.ds(points + l, LANES)] = spectrum[UNITS][0].astype(bf16)
        for k in range(1, UNITS):
            re, im = spectrum[k]
            c = cos_ref[k : k + 1, pl.ds(l, LANES)]
            s = sin_ref[k : k + 1, pl.ds(l, LANES)]
            z_ref[k, here, pl.ds(l, LANES)] = (re * c + im * s).astype(bf16)
            z_ref[k, here, pl.ds(points + l, LANES)] = (im * c - re * s).astype(bf16)
        return carry

    lax.fori_loop(0, rows // 16 * tiles, tile, 0)
    for h in range(HALVES):
        z = z_ref[h * GROUP : (h + 1) * GROUP].reshape(GROUP * rows, 2 * points)
        lobe = jnp.dot(z, mix_ref[...], preferred_element_type=f32)
        outs[h][...] = lobe.astype(bf16).reshape(GROUP, rows, 2 * LANES)
    outs[0][0] = jnp.dot(z_ref[0], real_ref[...], preferred_element_type=f32).astype(bf16)


def row_forward(fringes, part, late, *held):
    rows, width = fringes.shape
    part_rows = rows // ROW_PARTS
    block = min(32, part_rows)
    steps = part_rows // block
    tables = forward_tables(width)
    operands = [fringes, *[jnp.asarray(t) for t in tables], *late]
    count = len(operands) - len(late)
    return launch(
        lambda *refs: forward_kernel(*refs[:count], *refs[count + len(late) :]),
        held,
        operands,
        grid=(steps,),
        in_specs=[pl.BlockSpec((block, width), lambda i: (part * steps + i, 0))]
        + [whole(t) for t in tables]
        + [pl.BlockSpec(memory_space=pl.ANY) for _ in late],
        out_specs=[
            pl.BlockSpec((GROUP, block, 2 * LANES), lambda i: (0, i, 0)),
            pl.BlockSpec((GROUP, block, 2 * LANES), lambda i: (0, part * steps + i, 0)),
        ],
        out_shape=[
            jax.ShapeDtypeStruct((GROUP, part_rows, 2 * LANES), bf16),
            jax.ShapeDtypeStruct((GROUP, rows, 2 * LANES), bf16),
        ],
        aliases={count: 1} if late else {},
        scratch_shapes=[pltpu.VMEM((UNITS, block, 2 * width // RADIX), bf16)],
        name="row_forward",
    )


def first_kernel(devices, x_ref, cos_ref, sin_ref, o_ref):
    rows = x_ref.shape[1]

    def step(i, carry):
        here = pl.ds(pl.multiple_of(i * 16, 16), 16)
        cos_tab = cos_ref[here, :]
        sin_tab = sin_ref[here, :]

        def load(e):
            return (x_ref[e, here, :LANES].astype(f32), x_ref[e, here, LANES:].astype(f32))

        coarse = [complex_fft([load(rho * 4 + gamma) for rho in range(4)], -1) for gamma in range(4)]
        for q in range(4):
            fine = [turn(coarse[gamma][q], -gamma * q, devices) for gamma in range(4)]
            fine = complex_fft(fine + [None] * (devices // 4 - 4), -1)
            for p in range(devices // 4):
                u = q + 4 * p
                re, im = fine[p]
                c = cos_tab[:, u : u + 1]
                s = sin_tab[:, u : u + 1]
                o_ref[u, here, :LANES] = (re * c + im * s).astype(bf16)
                o_ref[u, here, LANES:] = (im * c - re * s).astype(bf16)
        return carry

    lax.fori_loop(0, rows // 16, step, 0)


def column_first(received, cos_tab, sin_tab, part, devices, *held):
    total = cos_tab.shape[0]
    rows = total // ROW_PARTS
    block = min(32, rows)
    steps = rows // block
    start = part * steps if received.shape[1] == total else 0
    table = pl.BlockSpec((block, devices), lambda i: (part * steps + i, 0))
    return launch(
        functools.partial(first_kernel, devices),
        held,
        [received, cos_tab, sin_tab],
        grid=(steps,),
        in_specs=[pl.BlockSpec((GROUP, block, 2 * LANES), lambda i: (0, start + i, 0)), table, table],
        out_specs=pl.BlockSpec((devices, block, 2 * LANES), lambda i: (0, i, 0)),
        out_shape=jax.ShapeDtypeStruct((devices, rows, 2 * LANES), bf16),
        name="column_first",
    )


def middle_kernel(*refs):
    parts, (forward_ref, inverse_ref, mask_ref, o_ref) = refs[:ROW_PARTS], refs[ROW_PARTS:]
    count = parts[0].shape[1]
    xs = [(ref[0, :, :LANES].astype(f32), ref[0, :, LANES:].astype(f32)) for ref in parts]
    mixed = complex_fft(xs, -1)
    folded_re, folded_im = [], []
    for q in range(ROW_PARTS):
        re, im = mixed[q][0].astype(bf16), mixed[q][1].astype(bf16)
        data = jnp.concatenate(
            [jnp.concatenate([re, im], axis=1), jnp.concatenate([im, -re], axis=1)], axis=0
        )
        spectrum = jnp.dot(forward_ref[q], data, preferred_element_type=f32) * mask_ref[...]
        folded = (spectrum[: count // 2] + spectrum[count // 2 :]).astype(bf16)
        folded_re.append(folded[:, :LANES])
        folded_im.append(folded[:, LANES:])
    re = jnp.concatenate(folded_re, axis=0)
    im = jnp.concatenate(folded_im, axis=0)
    data = jnp.concatenate(
        [jnp.concatenate([re, im], axis=1), jnp.concatenate([-im, re], axis=1)], axis=0
    )
    o_ref[0] = jnp.dot(inverse_ref[...], data, preferred_element_type=f32).astype(bf16)


def column_middle(parts, mask, *held):
    devices, part_rows, _ = parts[0].shape
    rows = part_rows * ROW_PARTS
    tables = column_tables(rows)
    piece = pl.BlockSpec((1, part_rows, 2 * LANES), lambda u: (u, 0, 0))
    return launch(
        middle_kernel,
        held,
        [*parts, *[jnp.asarray(t) for t in tables], mask],
        grid=(devices,),
        in_specs=[piece] * ROW_PARTS + [whole(t) for t in tables] + [whole(mask)],
        out_specs=pl.BlockSpec((1, rows // 2, 2 * LANES), lambda u: (u, 0, 0)),
        out_shape=jax.ShapeDtypeStruct((devices, rows // 2, 2 * LANES), bf16),
        name="column_middle",
    )


def last_kernel(devices, groups, group_ref, x_ref, cos_ref, sin_ref, *outs):
    rows = x_ref.shape[1]
    columns = devices // 4

    def step(i, carry):
        here = pl.ds(pl.multiple_of(i * 16, 16), 16)
        cos_tab = cos_ref[here, :]
        sin_tab = sin_ref[here, :]
        xs = []
        for u in range(devices):
            re = x_ref[u, here, :LANES].astype(f32)
            im = x_ref[u, here, LANES:].astype(f32)
            c = cos_tab[:, u : u + 1]
            s = sin_tab[:, u : u + 1]
            xs.append((re * c - im * s, im * c + re * s))
        ys = complex_fft(xs, 1)
        for delta in range(groups):
            carry_over = (group_ref[0] + delta) // groups
            for rho in range(4):
                for gamma in range(4):
                    re, im = ys[columns * rho + 4 * delta + gamma]
                    e = (rho + carry_over) % 4 * 4 + gamma if delta else rho * 4 + gamma
                    outs[delta][e, here, :LANES] = re.astype(bf16)
                    outs[delta][e, here, LANES:] = im.astype(bf16)
        return carry

    lax.fori_loop(0, rows // 16, step, 0)


def column_last(terms, cos_tab, sin_tab, group, part, groups, *held):
    devices, total, _ = terms.shape
    rows = total // ROW_PARTS
    block = min(32, rows)
    steps = rows // block
    table = pl.BlockSpec((block, devices), lambda i: (part * steps + i, 0))
    return launch(
        functools.partial(last_kernel, devices, groups),
        held,
        [group, terms, cos_tab, sin_tab],
        grid=(steps,),
        in_specs=[
            pl.BlockSpec(memory_space=pltpu.SMEM),
            pl.BlockSpec((devices, block, 2 * LANES), lambda i: (0, part * steps + i, 0)),
            table,
            table,
        ],
        out_specs=[pl.BlockSpec((GROUP, block, 2 * LANES), lambda i: (0, i, 0))] * groups,
        out_shape=[jax.ShapeDtypeStruct((GROUP, rows, 2 * LANES), bf16)] * groups,
        name="column_last",
    )


def sum_kernel(*refs):
    o_ref = refs[-1]
    count = len(refs) // HALVES
    for h in range(HALVES):
        total = refs[h * count][...].astype(f32)
        for ref in refs[h * count + 1 : (h + 1) * count]:
            total = total + ref[...].astype(f32)
        o_ref[:, h] = total.astype(bf16)


def add(pieces, *held):
    operands = [piece for shares in pieces for piece in shares]
    members, rows, lanes = operands[0].shape
    block = 4
    return launch(
        sum_kernel,
        held,
        operands,
        grid=(members // block,),
        in_specs=[pl.BlockSpec((block, rows, lanes), lambda i: (i, 0, 0))] * len(operands),
        out_specs=pl.BlockSpec((block, HALVES, rows, lanes), lambda i: (i, 0, 0, 0)),
        out_shape=jax.ShapeDtypeStruct((members, HALVES, rows, lanes), bf16),
        name="sum_shares",
    )


def inverse_kernel(first_block, per_device, zone_ref, table_ref, field_ref, *refs):
    cos_ref, sin_ref, mix_ref = refs[:3]
    o_ref, token_ref, g_ref = refs[-3:]
    token_ref[...] = jnp.zeros_like(token_ref)
    rows, width = o_ref.shape
    points = width // RADIX
    block = first_block + pl.program_id(0)
    field = field_ref[...].reshape(UNITS * rows, 2 * LANES)
    g_ref[...] = jnp.dot(field, mix_ref[...], preferred_element_type=f32).reshape(
        UNITS, rows, 4 * points
    )

    def tile(i, carry):
        l = pl.multiple_of(i * LANES, LANES)

        def load(residue):
            if residue in (0, UNITS):
                unit, second = 0, residue != 0
            else:
                unit, second = (residue, False) if residue < UNITS else (RADIX - residue, True)
            unit = unit % GROUP * HALVES + unit // GROUP
            start = 2 * points if second else 0
            re = g_ref[unit, :, pl.ds(start + l, LANES)]
            im = g_ref[unit, :, pl.ds(start + points + l, LANES)]
            if residue == 0:
                return (re, im)
            c = cos_ref[residue : residue + 1, pl.ds(l, LANES)]
            s = sin_ref[residue : residue + 1, pl.ds(l, LANES)]
            return (re * c - im * s, im * c + re * s)

        pixels = complex_fft([load(residue) for residue in range(RADIX)], 1)
        for p in range(RADIX):
            re, im = pixels[p]
            power = jnp.maximum(re * re + im * im, DAMPING_FLOOR * DAMPING_FLOOR)
            sine = im * lax.rsqrt(power)
            zone = zone_ref[block * RADIX + p]
            base = zone // per_device * (4 * per_device) + zone % per_device
            e = [table_ref[base + r * per_device] for r in range(4)]
            height = e[0] + sine * (e[1] + sine * (e[2] + sine * e[3]))
            o_ref[:, pl.ds(p * points + l, LANES)] = height.astype(bf16)
        return carry

    lax.fori_loop(0, points // LANES, tile, 0)


def row_inverse(field, zones, table, previous, part, shape, per_device, *held):
    part_rows = field.shape[2]
    rows, width = shape
    steps = part_rows // ZB_R
    tables = inverse_tables(width)
    smem = pl.BlockSpec(memory_space=pltpu.SMEM)
    extra = [] if previous is None else [previous]
    operands = [zones, table, field, *[jnp.asarray(t) for t in tables], *extra]
    return launch(
        functools.partial(inverse_kernel, part * steps, per_device),
        held,
        operands,
        grid=(steps,),
        in_specs=[smem, smem]
        + [pl.BlockSpec((GROUP, HALVES, ZB_R, 2 * LANES), lambda i: (0, 0, i, 0))]
        + [whole(t) for t in tables]
        + [pl.BlockSpec(memory_space=pl.ANY) for _ in extra],
        out_specs=[
            pl.BlockSpec((ZB_R, width), lambda i: (part * steps + i, 0)),
            pl.BlockSpec((8, LANES), lambda i: (0, 0)),
        ],
        out_shape=[jax.ShapeDtypeStruct(shape, bf16), jax.ShapeDtypeStruct((8, LANES), f32)],
        scratch_shapes=[pltpu.VMEM((UNITS, ZB_R, 4 * width // RADIX), f32)],
        aliases={len(operands) - 1: 0} if extra else {},
        name="row_inverse",
    )


def phase_table(rows, devices, offset, period):
    row = jnp.arange(rows, dtype=jnp.int32)[:, None] + offset
    turns = row * jnp.arange(devices, dtype=jnp.int32)[None, :] % period
    angles = turns.astype(f32) * (2.0 * math.pi / period)
    return jnp.cos(angles), jnp.sin(angles)


def body(groups, fringes, lobe_bounds, zone_index, zone_table):
    rows, width = fringes.shape
    devices = groups * GROUP
    height = rows * devices
    every = ("row", "group", "member")
    inside = ("row", "member")
    group = lax.axis_index("group")
    member = lax.axis_index(inside)

    def exchange(block):
        return lax.all_to_all(block, inside, split_axis=0, concat_axis=0, tiled=True)

    per_device = zone_table.shape[1]
    spread = jnp.broadcast_to(zone_table[None], (devices, 4, per_device))
    table = lax.all_to_all(spread, every, split_axis=0, concat_axis=0, tiled=True).reshape(-1)
    zones = zone_index.reshape(-1)

    first_offset = 4 * group * rows
    forward_phase = phase_table(rows, devices, first_offset, height)
    inverse_phase = phase_table(rows // 2, devices, first_offset // 2, height // 2)

    part_list = range(ROW_PARTS)
    masks = []
    for h in range(HALVES):
        columns = unit_columns(member + h * GROUP)
        keep = (columns[None, :] >= lobe_bounds[:, :1]) & (columns[None, :] < lobe_bounds[:, 1:])
        keep = keep.astype(f32) * (1.0 / (height * width))
        masks.append(jnp.repeat(jnp.tile(keep, (1, 2)), rows // ROW_PARTS // keep.shape[0], axis=0))

    lobes, late, arrived = [], [], []
    for part in part_list:
        held = [lobes[-1]] if part >= 1 else []
        if part >= 2:
            held.append(arrived[part - 2])
        lobe, *late = row_forward(fringes, part, late, *held)
        lobes.append(lobe)
        arrived.append(exchange(lobe))
    arrived_late = exchange(late[0])
    firsts = [[], []]
    last = lobes[-1]
    for part in part_list:
        last = column_first(arrived[part], *forward_phase, part, devices, last)
        firsts[0].append(last)
    terms = [column_middle(firsts[0], masks[0])]

    def send(pieces):
        return [
            lax.ppermute(pieces[d], "group", [(g, (g + d) % groups) for g in range(groups)])
            for d in range(1, groups)
        ]

    shares = []

    def finish(index, before):
        h, part = index // ROW_PARTS, index % ROW_PARTS
        held = [before] + (shares[index - 2][1:] if index >= 2 else [])
        pieces = column_last(terms[h], *inverse_phase, group.reshape(1), part, groups, *held)
        shares.append([pieces[0], *send(pieces)])
        return pieces[0]

    last = terms[0]
    for part in part_list:
        last = finish(part, last)
        if part % 2 == 1:
            for other in (part - 1, part):
                last = column_first(arrived_late, *forward_phase, other, devices, last)
                firsts[1].append(last)
    terms.append(column_middle(firsts[1], masks[1], last))
    last = terms[1]
    fields, result, token = [], None, None

    def gather(part, before):
        total = add([shares[part], shares[ROW_PARTS + part]], before)
        fields.append(exchange(total))
        return total

    for part in part_list:
        last = finish(ROW_PARTS + part, last)
        if part >= 2:
            last = gather(part - 2, last)
    for part in part_list:
        result, token = row_inverse(
            fields[part], zones, table, result, part, (rows // 2, width), per_device, last
        )
        last = token
        if part + 2 < ROW_PARTS:
            last = gather(part + 2, last)
    return result


def solution(mesh):
    row_size, col_size = mesh.shape["row"], mesh.shape["col"]
    groups = row_size * col_size // GROUP
    split = Mesh(
        mesh.devices.reshape(row_size, groups, col_size // groups), ("row", "group", "member")
    )
    every = ("row", "group", "member")
    placed = (P(every, None), P(), P(every, None), P(None, every))
    return jax.shard_map(
        functools.partial(body, groups),
        mesh=split,
        in_specs=placed,
        out_specs=P(every, None),
        check_vma=False,
    )
```

time: 1700 us -> 779 us (0.46)
  matrix products: 490 us -> 0 us
  Pallas kernels: 0 us -> 483 us
  local copies, waits for them, and re-layouts: 375 us -> 15.3 us
  blocking collectives: 243 us -> 31.5 us
  waiting for transfers between devices: 366 us -> 155 us
  other arithmetic: 182 us -> 5.96 us
  starting transfers between devices: 23.4 us -> 82.8 us
    dot_general x369 -> x0, matrix products: 490 us -> none  [the longest x84 118 us: complex_mix(): jnp.einsum(pattern, imag_part, sine_part, preferred_element_type=jnp.floa...]
    pallas_call x0 -> x30, Pallas kernels: none -> 483 us  [launch(): pl.pallas_call(lambda *refs: kernel(*refs[count:]), in_specs=[pl.BlockSpe...]
    all_to_all x2 -> x9, waiting for transfers between devices: 366 us -> 38.5 us  [the longest x8 38.5 us: exchange(): lax.all_to_all(block, inside, split_axis=0, concat_axis=0, tiled=True)]
    all_gather x1 -> x0, blocking collectives: 243 us -> none  [body(): full_table = lax.all_gather(zone_table, ('row', 'col'), axis=1, tiled=True)]
    while x369 -> x0, local copies, waits for them, and re-layouts: 180 us -> none
    ppermute x0 -> x8, waiting for transfers between devices: none -> 117 us  [send(): lax.ppermute(pieces[d], 'group', [(g, (g + d) % groups) for g in range(gr...]
    dynamic_update_slice x48 -> x0, other arithmetic: 88.3 us -> none  [the longest x32 71.6 us: height_block(): lax.dynamic_update_slice_in_dim(buffer, row_inverse(segment, block_coeffi...]
    another operation x38 -> x2, local copies, waits for them, and re-layouts: 85.6 us -> 0.05 us  [body(): jnp.tile(keep, (1, 2))]
  transfers between devices with their start and end apart: 2 -> 17, of which waited for: 1 -> 7; matrix products, arithmetic and copies ran while one was open for 0% -> 1% of each run, Pallas kernels for 0% -> 53%
where the time goes in v1:
time: 779 us; the launch traced here: 774 us
  Pallas kernels  483 us (62%)
  waiting for transfers between devices  155 us (20%)
  starting transfers between devices  82.8 us (11%)
  blocking collectives  31.5 us (4%)
  local copies, waits for them, and re-layouts  15.3 us (2%)
    pallas_call x30, Pallas kernels, launch(): pl.pallas_call(lambda *refs: kernel(*refs[count:]), in_specs=[pl.BlockSpe...  483 us
    ppermute x8, waiting for transfers between devices, send(): lax.ppermute(pieces[d], 'group', [(g, (g + d) % groups) for g in range(gr...  117 us
    all_to_all x8, starting transfers between devices, exchange(): lax.all_to_all(block, inside, split_axis=0, concat_axis=0, tiled=True)  47.4 us
    all_to_all x8, waiting for transfers between devices, exchange(): lax.all_to_all(block, inside, split_axis=0, concat_axis=0, tiled=True)  38.5 us
    all_to_all x1, blocking collectives, exchange(): lax.all_to_all(block, inside, split_axis=0, concat_axis=0, tiled=True)  31.5 us
    all_to_all x1, starting transfers between devices, body(): lax.all_to_all(spread, every, split_axis=0, concat_axis=0, tiled=True)  23.7 us
  transfers between devices with their start and end apart: 17, of which 7 were waited for; matrix products, arithmetic and copies ran while one was open for 1% of the time, Pallas kernels for 53%

profile of v1, /device:TPU:0, one launch (start us, length us, event | category | flops | bytes accessed | tf_op | source)
XLA Modules:
  0.0 774.1 jit_solution(16241994583578628011)
XLA Ops:
  0.0 32.6 %row_forward.4 = (bf16[16,256,256]{2,1,0:T(8,128)(2,1)}, bf16[16,1024,256]{2,1,0:T(8,128)(2,1)}) custom-call(bf16[1024,32768]{1,0:T(8,128)(2,1)} %refs_2_.5, f32[32,512]{1,0:T(8,128)} %constant.110.clone.refs_1_.refs_2_.refs_3_, f32[32,512]{1,0:T(8,128)} %constant.111.clone.refs_2_.refs_3_.refs_4_, ...), custom_call_target="tpu_custom_call" | custom-call | flops 1 | bytes 1 | tf_op jit(solution)/shard_map/row_forward/pallas_call | solution.py:202
  38.9 32.7 %row_forward.5 = (bf16[16,256,256]{2,1,0:T(8,128)(2,1)}, bf16[16,1024,256]{2,1,0:T(8,128)(2,1)}) custom-call(bf16[16,256,256]{2,1,0:T(8,128)(2,1)} %get-tuple-element.36.refs_0_, bf16[1024,32768]{1,0:T(8,128)(2,1)} %refs_2_.5, f32[32,512]{1,0:T(8,128)} %constant.110.clone.refs_1_.refs_2_.refs_3_, ...), custom_call_target="tpu_custom_call", output_to_operand_aliasing={{1}: (6, {})} | custom-call | flops 1 | bytes 1 | tf_op jit(solution)/shard_map/row_forward/pallas_call | solution.py:202
  76.9 32.7 %row_forward.6 = (bf16[16,256,256]{2,1,0:T(8,128)(2,1)}, bf16[16,1024,256]{2,1,0:T(8,128)(2,1)}) custom-call(bf16[16,256,256]{2,1,0:T(8,128)(2,1)} %get-tuple-element.38.refs_0_, bf16[16,256,256]{2,1,0:T(8,128)(2,1)} %copy-done, bf16[1024,32768]{1,0:T(8,128)(2,1)} %refs_2_.5, ...), custom_call_target="tpu_custom_call", output_to_operand_aliasing={{1}: (7, {})} | custom-call | flops 1 | bytes 1 | tf_op jit(solution)/shard_map/row_forward/pallas_call | solution.py:202
  114.7 32.7 %row_forward.7 = (bf16[16,256,256]{2,1,0:T(8,128)(2,1)}, bf16[16,1024,256]{2,1,0:T(8,128)(2,1)}) custom-call(bf16[16,256,256]{2,1,0:T(8,128)(2,1)} %get-tuple-element.40.refs_0_, bf16[16,256,256]{2,1,0:T(8,128)(2,1)} %all-to-all-done.1.refs_1_, bf16[1024,32768]{1,0:T(8,128)(2,1)} %refs_2_.5, ...), custom_call_target="tpu_custom_call", output_to_operand_aliasing={{1}: (7, {})} | custom-call | flops 1 | bytes 1 | tf_op jit(solution)/shard_map/row_forward/pallas_call | solution.py:202
  147.4 31.5 %all_to_all.50.refs_1_ = bf16[16,256,256]{2,1,0:T(8,128)(2,1)} all-to-all(bf16[16,256,256]{2,1,0:T(8,128)(2,1)} %get-tuple-element.42.refs_0_), channel_id=1, replica_groups=mesh['row'=4,'group'=2,'member'=4] {'row','member'}, dimensions={0} | all-to-all | bytes 4194304 | tf_op jit(solution)/shard_map/all_to_all | solution.py:530
  189.3 8.0 %column_first.8.refs_0_ = bf16[32,256,256]{2,1,0:T(8,128)(2,1)} custom-call(bf16[16,256,256]{2,1,0:T(8,128)(2,1)} %get-tuple-element.42.refs_0_, bf16[16,256,256]{2,1,0:T(8,128)(2,1)} %copy-done, f32[1024,32]{1,0:T(8,128)} %get-tuple-element.68.refs_2_, f32[1024,32]{1,0:T(8,128)} %get-tuple-element.67.refs_3_), custom_call_target="tpu_custom_call" | custom-call | flops 1 | bytes 1 | tf_op jit(solution)/shard_map/column_first/pallas_call | solution.py:202
  197.4 8.1 %column_first.9.refs_0_.refs_1_ = bf16[32,256,256]{2,1,0:T(8,128)(2,1)} custom-call(bf16[32,256,256]{2,1,0:T(8,128)(2,1)} %column_first.8.refs_0_, bf16[16,256,256]{2,1,0:T(8,128)(2,1)} %all-to-all-done.1.refs_1_, f32[1024,32]{1,0:T(8,128)} %get-tuple-element.68.refs_2_, f32[1024,32]{1,0:T(8,128)} %get-tuple-element.67.refs_3_), custom_call_target="tpu_custom_call" | custom-call | flops 1 | bytes 1 | tf_op jit(solution)/shard_map/column_first/pallas_call | solution.py:202
  205.5 8.0 %column_first.10.refs_0_.refs_2_ = bf16[32,256,256]{2,1,0:T(8,128)(2,1)} custom-call(bf16[32,256,256]{2,1,0:T(8,128)(2,1)} %column_first.9.refs_0_.refs_1_, bf16[16,256,256]{2,1,0:T(8,128)(2,1)} %copy-done.4, f32[1024,32]{1,0:T(8,128)} %get-tuple-element.68.refs_2_, f32[1024,32]{1,0:T(8,128)} %get-tuple-element.67.refs_3_), custom_call_target="tpu_custom_call" | custom-call | flops 1 | bytes 1 | tf_op jit(solution)/shard_map/column_first/pallas_call | solution.py:202
  214.3 8.0 %column_first.11.refs_3_ = bf16[32,256,256]{2,1,0:T(8,128)(2,1)} custom-call(bf16[32,256,256]{2,1,0:T(8,128)(2,1)} %column_first.10.refs_0_.refs_2_, bf16[16,256,256]{2,1,0:T(8,128)(2,1)} %all_to_all.50.refs_1_, f32[1024,32]{1,0:T(8,128)} %get-tuple-element.68.refs_2_, f32[1024,32]{1,0:T(8,128)} %get-tuple-element.67.refs_3_), custom_call_target="tpu_custom_call" | custom-call | flops 1 | bytes 1 | tf_op jit(solution)/shard_map/column_first/pallas_call | solution.py:202
  222.4 34.1 %column_middle.2.refs_0_.refs_2_.refs_3_ = bf16[32,512,256]{2,1,0:T(8,128)(2,1)} custom-call(bf16[32,256,256]{2,1,0:T(8,128)(2,1)} %column_first.8.refs_0_, bf16[32,256,256]{2,1,0:T(8,128)(2,1)} %column_first.9.refs_0_.refs_1_, bf16[32,256,256]{2,1,0:T(8,128)(2,1)} %column_first.10.refs_0_.refs_2_, bf16[32,256,256]{2,1,0:T(8,128)(2,1)} %column_first.11.refs_3_, ...), custom_call_target="tpu_custom_call" | custom-call | flops 1 | bytes 1 | tf_op jit(solution)/shard_map/column_middle/pallas_call | solution.py:202
  270.5 38.5 %all-to-all-done.4.refs_1_ = bf16[16,1024,256]{2,1,0:T(8,128)(2,1)} async-done(((bf16[16,1024,256]{2,1,0:T(8,128)(2,1)}), bf16[16,1024,256]{2,1,0:T(8,128)(2,1)}, u32[]{:S(2)}, u32[]{:S(2)}) %all-to-all-start.4) | async-done | bytes 8388640 | tf_op jit(solution)/shard_map/all_to_all | solution.py:530
  309.0 8.0 %column_first.12.refs_0_.refs_1_ = bf16[32,256,256]{2,1,0:T(8,128)(2,1)} custom-call(bf16[16,128,256]{2,1,0:T(8,128)(2,1)} %get-tuple-element.44.refs_0_.refs_1_, bf16[16,1024,256]{2,1,0:T(8,128)(2,1)} %all-to-all-done.4.refs_1_, f32[1024,32]{1,0:T(8,128)} %get-tuple-element.68.refs_2_, f32[1024,32]{1,0:T(8,128)} %get-tuple-element.67.refs_3_), custom_call_target="tpu_custom_call" | custom-call | flops 1 | bytes 1 | tf_op jit(solution)/shard_map/column_first/pallas_call | solution.py:202
  317.0 8.0 %column_first.13.refs_0_.refs_2_ = bf16[32,256,256]{2,1,0:T(8,128)(2,1)} custom-call(bf16[32,256,256]{2,1,0:T(8,128)(2,1)} %column_first.12.refs_0_.refs_1_, bf16[16,1024,256]{2,1,0:T(8,128)(2,1)} %all-to-all-done.4.refs_1_, f32[1024,32]{1,0:T(8,128)} %get-tuple-element.68.refs_2_, f32[1024,32]{1,0:T(8,128)} %get-tuple-element.67.refs_3_), custom_call_target="tpu_custom_call" | custom-call | flops 1 | bytes 1 | tf_op jit(solution)/shard_map/column_first/pallas_call | solution.py:202
  325.0 9.1 %collective-permute-done.refs_1_.refs_2_ = bf16[16,128,256]{2,1,0:T(8,128)(2,1)S(1)} collective-permute-done((bf16[16,128,256]{2,1,0:T(8,128)(2,1)}, bf16[16,128,256]{2,1,0:T(8,128)(2,1)S(1)}, u32[]{:S(2)}, u32[]{:S(2)}) %collective-permute-start) | collective-permute-done | bytes 1048608 | tf_op jit(solution)/shard_map/ppermute | solution.py:567
  340.7 27.1 %collective-permute-done.1.refs_1_.refs_2_ = bf16[16,128,256]{2,1,0:T(8,128)(2,1)S(1)} collective-permute-done((bf16[16,128,256]{2,1,0:T(8,128)(2,1)}, bf16[16,128,256]{2,1,0:T(8,128)(2,1)S(1)}, u32[]{:S(2)}, u32[]{:S(2)}) %collective-permute-start.1) | collective-permute-done | bytes 1048608 | tf_op jit(solution)/shard_map/ppermute | solution.py:567
  374.4 8.0 %column_first.14.refs_0_.refs_3_ = bf16[32,256,256]{2,1,0:T(8,128)(2,1)} custom-call(bf16[16,128,256]{2,1,0:T(8,128)(2,1)} %get-tuple-element.49.refs_0_.refs_1_, bf16[16,1024,256]{2,1,0:T(8,128)(2,1)} %all-to-all-done.4.refs_1_, f32[1024,32]{1,0:T(8,128)} %get-tuple-element.68.refs_2_, f32[1024,32]{1,0:T(8,128)} %get-tuple-element.67.refs_3_), custom_call_target="tpu_custom_call" | custom-call | flops 1 | bytes 1 | tf_op jit(solution)/shard_map/column_first/pallas_call | solution.py:202
  391.2 34.1 %column_middle.3.refs_0_.refs_3_ = bf16[32,512,256]{2,1,0:T(8,128)(2,1)} custom-call(bf16[32,256,256]{2,1,0:T(8,128)(2,1)} %column_first.15.refs_0_.refs_4_, bf16[32,256,256]{2,1,0:T(8,128)(2,1)} %column_first.12.refs_0_.refs_1_, bf16[32,256,256]{2,1,0:T(8,128)(2,1)} %column_first.13.refs_0_.refs_2_, bf16[32,256,256]{2,1,0:T(8,128)(2,1)} %column_first.14.refs_0_.refs_3_, ...), custom_call_target="tpu_custom_call" | custom-call | flops 1 | bytes 1 | tf_op jit(solution)/shard_map/column_middle/pallas_call | solution.py:202
  435.5 23.7 %all-to-all-start.5 = ((f32[32,1,128]{2,1,0:T(1,128)}), f32[32,1,128]{2,1,0:T(1,128)S(1)}, u32[]{:S(2)}, u32[]{:S(2)}) async-start(f32[32,1,128]{2,1,0:T(1,128)} %reshape.174), calls=%async_computation.5 | async-start | bytes 32768 | tf_op jit(solution)/shard_map/all_to_all | solution.py:534
  465.7 25.1 %collective-permute-done.4.refs_1_.refs_4_ = bf16[16,128,256]{2,1,0:T(8,128)(2,1)S(1)} collective-permute-done((bf16[16,128,256]{2,1,0:T(8,128)(2,1)}, bf16[16,128,256]{2,1,0:T(8,128)(2,1)S(1)}, u32[]{:S(2)}, u32[]{:S(2)}) %collective-permute-start.4) | collective-permute-done | bytes 1048608 | tf_op jit(solution)/shard_map/ppermute | solution.py:567
  511.0 46.3 %collective-permute-done.5.refs_1_.refs_4_ = bf16[16,128,256]{2,1,0:T(8,128)(2,1)S(1)} collective-permute-done((bf16[16,128,256]{2,1,0:T(8,128)(2,1)S(1)}, bf16[16,128,256]{2,1,0:T(8,128)(2,1)S(1)}, u32[]{:S(2)}, u32[]{:S(2)}) %collective-permute-start.5) | collective-permute-done | bytes 1048608 | tf_op jit(solution)/shard_map/ppermute | solution.py:567
  579.8 39.5 %row_inverse.4 = (bf16[512,32768]{1,0:T(8,128)(2,1)}, f32[8,128]{1,0:T(8,128)}) custom-call(bf16[16,2,128,256]{3,2,1,0:T(8,128)(2,1)} %sum_shares.5.refs_0_, s32[2048]{0:T(1024)} %reshape.172.refs_1_, f32[4096]{0:T(1024)} %reshape.173.refs_2_, bf16[16,2,128,256]{3,2,1,0:T(8,128)(2,1)} %copy-done.3, f32[64,512]{1,0:T(8,128)} %constant.116.clone.refs_4_, ...), custom_call_target="tpu_custom_call" | custom-call | flops 1 | bytes 1 | tf_op jit(solution)/shard_map/row_inverse/pallas_call | solution.py:202
  636.8 39.6 %row_inverse.5 = (bf16[512,32768]{1,0:T(8,128)(2,1)}, f32[8,128]{1,0:T(8,128)}) custom-call(bf16[16,2,128,256]{3,2,1,0:T(8,128)(2,1)} %sum_shares.6.refs_0_, s32[2048]{0:T(1024)} %reshape.172.refs_1_, f32[4096]{0:T(1024)} %reshape.173.refs_2_, bf16[16,2,128,256]{3,2,1,0:T(8,128)(2,1)} %copy-done.1, ...), custom_call_target="tpu_custom_call", output_to_operand_aliasing={{0}: (7, {})} | custom-call | flops 1 | bytes 1 | tf_op jit(solution)/shard_map/row_inverse/pallas_call | solution.py:202
  693.6 39.6 %row_inverse.6 = (bf16[512,32768]{1,0:T(8,128)(2,1)}, f32[8,128]{1,0:T(8,128)}) custom-call(bf16[16,2,128,256]{3,2,1,0:T(8,128)(2,1)} %sum_shares.7.refs_0_, s32[2048]{0:T(1024)} %reshape.172.refs_1_, f32[4096]{0:T(1024)} %reshape.173.refs_2_, bf16[16,2,128,256]{3,2,1,0:T(8,128)(2,1)} %all-to-all-done.8.refs_3_, ...), custom_call_target="tpu_custom_call", output_to_operand_aliasing={{0}: (7, {})} | custom-call | flops 1 | bytes 1 | tf_op jit(solution)/shard_map/row_inverse/pallas_call | solution.py:202
  734.5 39.6 %row_inverse.7 = (bf16[512,32768]{1,0:T(8,128)(2,1)}, f32[8,128]{1,0:T(8,128)}) custom-call(f32[8,128]{1,0:T(8,128)} %get-tuple-element.64.refs_0_, s32[2048]{0:T(1024)} %reshape.172.refs_1_, f32[4096]{0:T(1024)} %reshape.173.refs_2_, bf16[16,2,128,256]{3,2,1,0:T(8,128)(2,1)} %copy-done.2, ...), custom_call_target="tpu_custom_call", output_to_operand_aliasing={{0}: (7, {})} | custom-call | flops 1 | bytes 1 | tf_op jit(solution)/shard_map/row_inverse/pallas_call | solution.py:202
  (99 shorter events, 159.0 us)
Async XLA Ops:
  32.6 39.0 %all-to-all-start = ((bf16[16,256,256]{2,1,0:T(8,128)(2,1)}), bf16[16,256,256]{2,1,0:T(8,128)(2,1)S(1)}, u32[]{:S(2)}, u32[]{:S(2)}) async-start(bf16[16,256,256]{2,1,0:T(8,128)(2,1)} %get-tuple-element.36.refs_0_), calls=%async_computation | async-start | bytes 4194304 | tf_op jit(solution)/shard_map/all_to_all | solution.py:530
  71.7 5.2 copy-start
  71.7 37.9 %all-to-all-start.1 = ((bf16[16,256,256]{2,1,0:T(8,128)(2,1)}), bf16[16,256,256]{2,1,0:T(8,128)(2,1)}, u32[]{:S(2)}, u32[]{:S(2)}) async-start(bf16[16,256,256]{2,1,0:T(8,128)(2,1)} %get-tuple-element.38.refs_0_), calls=%async_computation.1 | async-start | bytes 4194304 | tf_op jit(solution)/shard_map/all_to_all | solution.py:530
  109.6 37.8 %all-to-all-start.2 = ((bf16[16,256,256]{2,1,0:T(8,128)(2,1)}), bf16[16,256,256]{2,1,0:T(8,128)(2,1)S(1)}, u32[]{:S(2)}, u32[]{:S(2)}) async-start(bf16[16,256,256]{2,1,0:T(8,128)(2,1)} %get-tuple-element.40.refs_0_), calls=%async_computation.2 | async-start | bytes 4194304 | tf_op jit(solution)/shard_map/all_to_all | solution.py:530
  147.4 31.5 %copy-start.4 = (bf16[16,256,256]{2,1,0:T(8,128)(2,1)}, bf16[16,256,256]{2,1,0:T(8,128)(2,1)S(1)}, u32[]{:S(2)}) copy-start(bf16[16,256,256]{2,1,0:T(8,128)(2,1)S(1)} %all-to-all-done.2.refs_1_) | copy-start | bytes 6291460
  178.9 130.0 %all-to-all-start.4 = ((bf16[16,1024,256]{2,1,0:T(8,128)(2,1)}), bf16[16,1024,256]{2,1,0:T(8,128)(2,1)}, u32[]{:S(2)}, u32[]{:S(2)}) async-start(bf16[16,1024,256]{2,1,0:T(8,128)(2,1)} %get-tuple-element.45), calls=%async_computation.4 | async-start | bytes 16777216 | tf_op jit(solution)/shard_map/all_to_all | solution.py:530
  262.0 72.1 %collective-permute-start = (bf16[16,128,256]{2,1,0:T(8,128)(2,1)}, bf16[16,128,256]{2,1,0:T(8,128)(2,1)S(1)}, u32[]{:S(2)}, u32[]{:S(2)}) collective-permute-start(bf16[16,128,256]{2,1,0:T(8,128)(2,1)} %get-tuple-element.46), channel_id=1, source_target_pairs={{0,4},{4,0},{1,5},{5,1},{2,6},{6,2},{3,7},{7,3},{8,12},{12,8},{9,1... | collective-permute-start | bytes 3145736 | tf_op jit(solution)/shard_map/ppermute | solution.py:567
  270.2 97.7 %collective-permute-start.1 = (bf16[16,128,256]{2,1,0:T(8,128)(2,1)}, bf16[16,128,256]{2,1,0:T(8,128)(2,1)S(1)}, u32[]{:S(2)}, u32[]{:S(2)}) collective-permute-start(bf16[16,128,256]{2,1,0:T(8,128)(2,1)} %get-tuple-element.48), channel_id=1, source_target_pairs={{0,4},{4,0},{1,5},{5,1},{2,6},{6,2},{3,7},{7,3},{8,12},{12,8},{9,1... | collective-permute-start | bytes 3145736 | tf_op jit(solution)/shard_map/ppermute | solution.py:567
  340.7 84.7 %collective-permute-start.2 = (bf16[16,128,256]{2,1,0:T(8,128)(2,1)}, bf16[16,128,256]{2,1,0:T(8,128)(2,1)S(1)}, u32[]{:S(2)}, u32[]{:S(2)}) collective-permute-start(bf16[16,128,256]{2,1,0:T(8,128)(2,1)} %get-tuple-element.50), channel_id=1, source_target_pairs={{0,4},{4,0},{1,5},{5,1},{2,6},{6,2},{3,7},{7,3},{8,12},{12,8},{9,1... | collective-permute-start | bytes 3145736 | tf_op jit(solution)/shard_map/ppermute | solution.py:567
  391.2 68.0 %collective-permute-start.3 = (bf16[16,128,256]{2,1,0:T(8,128)(2,1)}, bf16[16,128,256]{2,1,0:T(8,128)(2,1)S(1)}, u32[]{:S(2)}, u32[]{:S(2)}) collective-permute-start(bf16[16,128,256]{2,1,0:T(8,128)(2,1)} %get-tuple-element.52), channel_id=1, source_target_pairs={{0,4},{4,0},{1,5},{5,1},{2,6},{6,2},{3,7},{7,3},{8,12},{12,8},{9,1... | collective-permute-start | bytes 3145736 | tf_op jit(solution)/shard_map/ppermute | solution.py:567
  425.3 9.5 %copy-start.14 = (f32[4,32]{1,0:T(4,128)S(1)}, f32[4,32]{1,0:T(4,128)}, u32[]{:S(2)}) copy-start(f32[4,32]{1,0:T(4,128)} %param.39) | copy-start | bytes 1540
  431.9 58.9 %collective-permute-start.4 = (bf16[16,128,256]{2,1,0:T(8,128)(2,1)}, bf16[16,128,256]{2,1,0:T(8,128)(2,1)S(1)}, u32[]{:S(2)}, u32[]{:S(2)}) collective-permute-start(bf16[16,128,256]{2,1,0:T(8,128)(2,1)} %get-tuple-element.54), channel_id=1, source_target_pairs={{0,4},{4,0},{1,5},{5,1},{2,6},{6,2},{3,7},{7,3},{8,12},{12,8},{9,1... | collective-permute-start | bytes 3145736 | tf_op jit(solution)/shard_map/ppermute | solution.py:567
  435.5 66.3 %all-to-all-start.5 = ((f32[32,1,128]{2,1,0:T(1,128)}), f32[32,1,128]{2,1,0:T(1,128)S(1)}, u32[]{:S(2)}, u32[]{:S(2)}) async-start(f32[32,1,128]{2,1,0:T(1,128)} %reshape.174), calls=%async_computation.5 | async-start | bytes 32768 | tf_op jit(solution)/shard_map/all_to_all | solution.py:534
  497.4 12.3 %copy-start.17 = (bf16[16,128,256]{2,1,0:T(8,128)(2,1)S(1)}, bf16[16,128,256]{2,1,0:T(8,128)(2,1)}, u32[]{:S(2)}) copy-start(bf16[16,128,256]{2,1,0:T(8,128)(2,1)} %get-tuple-element.56) | copy-start | bytes 3145732
  501.8 66.5 %all-to-all-start.6 = ((bf16[16,2,128,256]{3,2,1,0:T(8,128)(2,1)}), bf16[16,2,128,256]{3,2,1,0:T(8,128)(2,1)S(1)}, u32[]{:S(2)}, u32[]{:S(2)}) async-start(bf16[16,2,128,256]{3,2,1,0:T(8,128)(2,1)} %sum_shares.4.refs_0_), calls=%async_computation.6 | async-start | bytes 4194304 | tf_op jit(solution)/shard_map/all_to_all | solution.py:530
  509.7 47.6 %collective-permute-start.5 = (bf16[16,128,256]{2,1,0:T(8,128)(2,1)S(1)}, bf16[16,128,256]{2,1,0:T(8,128)(2,1)S(1)}, u32[]{:S(2)}, u32[]{:S(2)}) collective-permute-start(bf16[16,128,256]{2,1,0:T(8,128)(2,1)S(1)} %copy-done.17), channel_id=1, source_target_pairs={{0,4},{4,0},{1,5},{5,1},{2,6},{6,2},{3,7},{7,3},{8,12},{12,8},{9,1... | collective-permute-start | bytes 3145736 | tf_op jit(solution)/shard_map/ppermute | solution.py:567
  563.9 13.2 %copy-start.13 = (s32[32,64]{1,0:T(8,128)S(1)}, s32[32,64]{1,0:T(8,128)}, u32[]{:S(2)}) copy-start(s32[32,64]{1,0:T(8,128)} %param.38) | copy-start | bytes 24580
  569.6 58.4 %all-to-all-start.7 = ((bf16[16,2,128,256]{3,2,1,0:T(8,128)(2,1)}), bf16[16,2,128,256]{3,2,1,0:T(8,128)(2,1)S(1)}, u32[]{:S(2)}, u32[]{:S(2)}) async-start(bf16[16,2,128,256]{3,2,1,0:T(8,128)(2,1)} %sum_shares.5.refs_0_), calls=%async_computation.7 | async-start | bytes 4194304 | tf_op jit(solution)/shard_map/all_to_all | solution.py:530
  575.0 47.7 %collective-permute-start.6 = (bf16[16,128,256]{2,1,0:T(8,128)(2,1)}, bf16[16,128,256]{2,1,0:T(8,128)(2,1)S(1)}, u32[]{:S(2)}, u32[]{:S(2)}) collective-permute-start(bf16[16,128,256]{2,1,0:T(8,128)(2,1)} %get-tuple-element.59), channel_id=1, source_target_pairs={{0,4},{4,0},{1,5},{5,1},{2,6},{6,2},{3,7},{7,3},{8,12},{12,8},{9,1... | collective-permute-start | bytes 3145736 | tf_op jit(solution)/shard_map/ppermute | solution.py:567
  628.0 6.3 copy-start.16
  628.0 8.8 %copy-start.1 = (bf16[16,2,128,256]{3,2,1,0:T(8,128)(2,1)}, bf16[16,2,128,256]{3,2,1,0:T(8,128)(2,1)S(1)}, u32[]{:S(2)}) copy-start(bf16[16,2,128,256]{3,2,1,0:T(8,128)(2,1)S(1)} %all-to-all-done.7.refs_3_) | copy-start | bytes 6291460
  628.0 59.2 %all-to-all-start.8 = ((bf16[16,2,128,256]{3,2,1,0:T(8,128)(2,1)}), bf16[16,2,128,256]{3,2,1,0:T(8,128)(2,1)}, u32[]{:S(2)}, u32[]{:S(2)}) async-start(bf16[16,2,128,256]{3,2,1,0:T(8,128)(2,1)} %sum_shares.6.refs_0_), calls=%async_computation.8 | async-start | bytes 4194304 | tf_op jit(solution)/shard_map/all_to_all | solution.py:530
  634.3 47.6 %collective-permute-start.7 = (bf16[16,128,256]{2,1,0:T(8,128)(2,1)S(1)}, bf16[16,128,256]{2,1,0:T(8,128)(2,1)S(1)}, u32[]{:S(2)}, u32[]{:S(2)}) collective-permute-start(bf16[16,128,256]{2,1,0:T(8,128)(2,1)S(1)} %copy-done.16), channel_id=1, source_target_pairs={{0,4},{4,0},{1,5},{5,1},{2,6},{6,2},{3,7},{7,3},{8,12},{12,8},{9,1... | collective-permute-start | bytes 3145736 | tf_op jit(solution)/shard_map/ppermute | solution.py:567
  687.2 46.0 %all-to-all-start.9 = ((bf16[16,2,128,256]{3,2,1,0:T(8,128)(2,1)}), bf16[16,2,128,256]{3,2,1,0:T(8,128)(2,1)S(1)}, u32[]{:S(2)}, u32[]{:S(2)}) async-start(bf16[16,2,128,256]{3,2,1,0:T(8,128)(2,1)} %sum_shares.7.refs_0_), calls=%async_computation.9 | async-start | bytes 4194304 | tf_op jit(solution)/shard_map/all_to_all | solution.py:530
  (11 other events, 16.0 us)

commit v2 on v1

--- a/solution.py
+++ b/solution.py
@@ -22,6 +22,7 @@
 HALVES = UNITS // GROUP
 LANES = 128
 ROW_PARTS = 4
+OUT_PARTS = (2, 2, 2, 2)
 
 f32 = jnp.float32
 bf16 = jnp.bfloat16
@@ -154,25 +155,25 @@
     points = width // RADIX
     per_residue = LOBE // RADIX
     b = np.arange(points)[:, None]
-    twist_cos, twist_sin = cos_sin(np.arange(UNITS)[:, None] * b.T, width)
+    twist_cos, twist_sin = cos_sin(np.arange(UNITS + 1)[:, None] * b.T, width)
     j = LOBE_START // RADIX + np.arange(per_residue)[None, :]
     c1, s1 = cos_sin(b * j, points)
     c2, s2 = cos_sin(b * (j + 1), points)
     mix = np.block([[c1, c2, -s1, -s2], [s1, -s2, c1, -c2]])
-    c3, s3 = cos_sin(b * (2 * j + 1), 2 * points)
-    zero = np.zeros_like(c1)
-    mix_real = np.block([[c1, zero, -s1, zero], [zero, c3, zero, -s3]])
-    return twist_cos.astype(np.float32), twist_sin.astype(np.float32), as_bf16(mix), as_bf16(mix_real)
+    return twist_cos.astype(np.float32), twist_sin.astype(np.float32), as_bf16(mix)
 
 
 def inverse_tables(width):
     points = width // RADIX
     per_residue = LOBE // RADIX
     q = np.arange(points)[None, :]
-    twist_cos, twist_sin = cos_sin(np.arange(RADIX)[:, None] * q, width)
-    c, s = cos_sin(np.arange(per_residue)[:, None] * q, points)
-    zero = np.zeros_like(c)
-    mix = np.block([[c, s, zero, zero], [zero, zero, c, s], [-s, c, zero, zero], [zero, zero, -s, c]])
+    residue = np.arange(UNITS)[:, None]
+    turns = np.concatenate([residue * q, residue * (q + points)])
+    twist_cos, twist_sin = cos_sin(turns, width)
+    column = np.arange(per_residue)[:, None]
+    c1, s1 = cos_sin(column * q, points)
+    c2, s2 = cos_sin((2 * column + 1) * q, 2 * points)
+    mix = np.block([[c1, s1, c1, s1], [c2, s2, -c2, -s2], [-s1, c1, -s1, c1], [-s2, c2, s2, -c2]])
     return twist_cos.astype(np.float32), twist_sin.astype(np.float32), as_bf16(mix)
 
 
@@ -190,6 +191,11 @@
     return as_bf16(np.stack(forward)), as_bf16(np.concatenate([c, s], axis=1))
 
 
+def out_part(part, rows):
+    eighth = rows // 8
+    return sum(OUT_PARTS[:part]) * eighth, OUT_PARTS[part] * eighth
+
+
 def unit_columns(unit):
     lane = jnp.arange(LANES, dtype=jnp.int32)
     per_residue = LOBE // RADIX
@@ -197,56 +203,81 @@
     return RADIX * (lane % per_residue) + jnp.where(lane < per_residue, unit, second)
 
 
-def launch(kernel, held, operands, in_specs, aliases=None, **options):
+def launch(kernel, held, operands, in_specs, aliases=None, cost=1, **options):
     count = len(held)
     return pl.pallas_call(
         lambda *refs: kernel(*refs[count:]),
         in_specs=[pl.BlockSpec(memory_space=pl.ANY)] * count + in_specs,
         input_output_aliases={count + k: v for k, v in (aliases or {}).items()},
         compiler_params=pltpu.CompilerParams(vmem_limit_bytes=VMEM_LIMIT),
-        cost_estimate=pl.CostEstimate(flops=1, bytes_accessed=1, transcendentals=0),
+        cost_estimate=pl.CostEstimate(flops=cost, bytes_accessed=cost, transcendentals=0),
         **options,
     )(*held, *operands)
 
 
+def gate(value, *held):
+    spec = pl.BlockSpec(memory_space=pl.ANY)
+    return launch(
+        lambda *refs: None,
+        held,
+        [value],
+        in_specs=[spec],
+        out_specs=spec,
+        out_shape=jax.ShapeDtypeStruct(value.shape, value.dtype),
+        aliases={0: 0},
+        name="gate",
+    )
+
+
 def whole(array):
     return pl.BlockSpec(array.shape, lambda *_: (0,) * array.ndim)
 
 
-def forward_kernel(x_ref, cos_ref, sin_ref, mix_ref, real_ref, *refs):
-    outs, z_ref = refs[:HALVES], refs[HALVES]
+def forward_kernel(x_ref, cos_ref, sin_ref, mix_ref, *refs):
+    outs, slots = refs[:HALVES], refs[HALVES:]
     rows, width = x_ref.shape
     points = width // RADIX
     tiles = points // LANES
-
-    def tile(i, carry):
-        r = pl.multiple_of((i // tiles) * 16, 16)
-        l = pl.multiple_of((i % tiles) * LANES, LANES)
+    lane = lax.broadcasted_iota(jnp.int32, (16, 2 * LANES), 1)
+    first_residue = lane % LANES < LANES // 2
+
+    def butterfly(z_ref, r, l):
         here = pl.ds(r, 16)
         xs = [x_ref[here, pl.ds(a * points + l, LANES)].astype(f32) for a in range(RADIX)]
         spectrum = real_fft(xs)
-        z_ref[0, here, pl.ds(l, LANES)] = spectrum[0][0].astype(bf16)
-        z_ref[0, here, pl.ds(points + l, LANES)] = spectrum[UNITS][0].astype(bf16)
-        for k in range(1, UNITS):
+        z_ref[0, :, pl.ds(l, LANES)] = spectrum[0][0].astype(bf16)
+        z_ref[0, :, pl.ds(points + l, LANES)] = jnp.zeros((16, LANES), bf16)
+        for k in range(1, UNITS + 1):
             re, im = spectrum[k]
             c = cos_ref[k : k + 1, pl.ds(l, LANES)]
             s = sin_ref[k : k + 1, pl.ds(l, LANES)]
-            z_ref[k, here, pl.ds(l, LANES)] = (re * c + im * s).astype(bf16)
-            z_ref[k, here, pl.ds(points + l, LANES)] = (im * c - re * s).astype(bf16)
-        return carry
-
-    lax.fori_loop(0, rows // 16 * tiles, tile, 0)
-    for h in range(HALVES):
-        z = z_ref[h * GROUP : (h + 1) * GROUP].reshape(GROUP * rows, 2 * points)
+            if im is None:
+                z_ref[k, :, pl.ds(l, LANES)] = (re * c).astype(bf16)
+                z_ref[k, :, pl.ds(points + l, LANES)] = (re * -s).astype(bf16)
+            else:
+                z_ref[k, :, pl.ds(l, LANES)] = (re * c + im * s).astype(bf16)
+                z_ref[k, :, pl.ds(points + l, LANES)] = (im * c - re * s).astype(bf16)
+
+    def mix(z_ref, r):
+        z = z_ref[...].reshape((UNITS + 1) * 16, 2 * points)
         lobe = jnp.dot(z, mix_ref[...], preferred_element_type=f32)
-        outs[h][...] = lobe.astype(bf16).reshape(GROUP, rows, 2 * LANES)
-    outs[0][0] = jnp.dot(z_ref[0], real_ref[...], preferred_element_type=f32).astype(bf16)
+        lobe = lobe.astype(bf16).reshape(UNITS + 1, 16, 2 * LANES)
+        here = pl.ds(r, 16)
+        outs[0][0, here] = jnp.where(first_residue, lobe[0], lobe[UNITS])
+        outs[0][1:, here] = lobe[1:GROUP]
+        for h in range(1, HALVES):
+            outs[h][:, here] = lobe[h * GROUP : (h + 1) * GROUP]
+
+    for g in range(rows // 16):
+        for t in range(tiles):
+            butterfly(slots[0], g * 16, t * LANES)
+        mix(slots[0], g * 16)
 
 
 def row_forward(fringes, part, late, *held):
     rows, width = fringes.shape
     part_rows = rows // ROW_PARTS
-    block = min(32, part_rows)
+    block = min(16, part_rows)
     steps = part_rows // block
     tables = forward_tables(width)
     operands = [fringes, *[jnp.asarray(t) for t in tables], *late]
@@ -268,7 +299,7 @@
             jax.ShapeDtypeStruct((GROUP, rows, 2 * LANES), bf16),
         ],
         aliases={count: 1} if late else {},
-        scratch_shapes=[pltpu.VMEM((UNITS, block, 2 * width // RADIX), bf16)],
+        scratch_shapes=[pltpu.VMEM((UNITS + 1, 16, 2 * width // RADIX), bf16)] * 2,
         name="row_forward",
     )
 
@@ -301,18 +332,17 @@
 
 
 def column_first(received, cos_tab, sin_tab, part, devices, *held):
-    total = cos_tab.shape[0]
-    rows = total // ROW_PARTS
-    block = min(32, rows)
+    total, rows = cos_tab.shape[0], received.shape[1]
+    block = min(64, total // ROW_PARTS)
     steps = rows // block
-    start = part * steps if received.shape[1] == total else 0
-    table = pl.BlockSpec((block, devices), lambda i: (part * steps + i, 0))
+    start = 0 if rows == total else part * steps
+    table = pl.BlockSpec((block, devices), lambda i: (start + i, 0))
     return launch(
         functools.partial(first_kernel, devices),
         held,
         [received, cos_tab, sin_tab],
         grid=(steps,),
-        in_specs=[pl.BlockSpec((GROUP, block, 2 * LANES), lambda i: (0, start + i, 0)), table, table],
+        in_specs=[pl.BlockSpec((GROUP, block, 2 * LANES), lambda i: (0, i, 0)), table, table],
         out_specs=pl.BlockSpec((devices, block, 2 * LANES), lambda i: (0, i, 0)),
         out_shape=jax.ShapeDtypeStruct((devices, rows, 2 * LANES), bf16),
         name="column_first",
@@ -322,38 +352,46 @@
 def middle_kernel(*refs):
     parts, (forward_ref, inverse_ref, mask_ref, o_ref) = refs[:ROW_PARTS], refs[ROW_PARTS:]
     count = parts[0].shape[1]
-    xs = [(ref[0, :, :LANES].astype(f32), ref[0, :, LANES:].astype(f32)) for ref in parts]
-    mixed = complex_fft(xs, -1)
-    folded_re, folded_im = [], []
-    for q in range(ROW_PARTS):
-        re, im = mixed[q][0].astype(bf16), mixed[q][1].astype(bf16)
+    for u in range(o_ref.shape[0]):
+        xs = [(ref[u, :, :LANES].astype(f32), ref[u, :, LANES:].astype(f32)) for ref in parts]
+        mixed = complex_fft(xs, -1)
+        folded_re, folded_im = [], []
+        for q in range(ROW_PARTS):
+            re, im = mixed[q][0].astype(bf16), mixed[q][1].astype(bf16)
+            data = jnp.concatenate(
+                [jnp.concatenate([re, im], axis=1), jnp.concatenate([im, -re], axis=1)], axis=0
+            )
+            spectrum = jnp.dot(forward_ref[q], data, preferred_element_type=f32) * mask_ref[...]
+            folded = (spectrum[: count // 2] + spectrum[count // 2 :]).astype(bf16)
+            folded_re.append(folded[:, :LANES])
+            folded_im.append(folded[:, LANES:])
+        re = jnp.concatenate(folded_re, axis=0)
+        im = jnp.concatenate(folded_im, axis=0)
         data = jnp.concatenate(
-            [jnp.concatenate([re, im], axis=1), jnp.concatenate([im, -re], axis=1)], axis=0
+            [jnp.concatenate([re, im], axis=1), jnp.concatenate([-im, re], axis=1)], axis=0
         )
-        spectrum = jnp.dot(forward_ref[q], data, preferred_element_type=f32) * mask_ref[...]
-        folded = (spectrum[: count // 2] + spectrum[count // 2 :]).astype(bf16)
-        folded_re.append(folded[:, :LANES])
-        folded_im.append(folded[:, LANES:])
-    re = jnp.concatenate(folded_re, axis=0)
-    im = jnp.concatenate(folded_im, axis=0)
-    data = jnp.concatenate(
-        [jnp.concatenate([re, im], axis=1), jnp.concatenate([-im, re], axis=1)], axis=0
-    )
-    o_ref[0] = jnp.dot(inverse_ref[...], data, preferred_element_type=f32).astype(bf16)
+        o_ref[u] = jnp.dot(inverse_ref[...], data, preferred_element_type=f32).astype(bf16)
 
 
 def column_middle(parts, mask, *held):
-    devices, part_rows, _ = parts[0].shape
-    rows = part_rows * ROW_PARTS
+    devices = parts[0].shape[0]
+    rows = sum(part.shape[1] for part in parts)
+    part_rows = rows // ROW_PARTS
+    block = 4
     tables = column_tables(rows)
-    piece = pl.BlockSpec((1, part_rows, 2 * LANES), lambda u: (u, 0, 0))
+    if len(parts) == 1:
+        parts = parts * ROW_PARTS
+        places = range(ROW_PARTS)
+    else:
+        places = [0] * ROW_PARTS
+    pieces = [pl.BlockSpec((block, part_rows, 2 * LANES), lambda u, r=r: (u, r, 0)) for r in places]
     return launch(
         middle_kernel,
         held,
         [*parts, *[jnp.asarray(t) for t in tables], mask],
-        grid=(devices,),
-        in_specs=[piece] * ROW_PARTS + [whole(t) for t in tables] + [whole(mask)],
-        out_specs=pl.BlockSpec((1, rows // 2, 2 * LANES), lambda u: (u, 0, 0)),
+        grid=(devices // block,),
+        in_specs=pieces + [whole(t) for t in tables] + [whole(mask)],
+        out_specs=pl.BlockSpec((block, rows // 2, 2 * LANES), lambda u: (u, 0, 0)),
         out_shape=jax.ShapeDtypeStruct((devices, rows // 2, 2 * LANES), bf16),
         name="column_middle",
     )
@@ -390,10 +428,11 @@
 
 def column_last(terms, cos_tab, sin_tab, group, part, groups, *held):
     devices, total, _ = terms.shape
-    rows = total // ROW_PARTS
-    block = min(32, rows)
+    first, rows = out_part(part, total)
+    block = min(64, rows)
     steps = rows // block
-    table = pl.BlockSpec((block, devices), lambda i: (part * steps + i, 0))
+    start = first // block
+    table = pl.BlockSpec((block, devices), lambda i: (start + i, 0))
     return launch(
         functools.partial(last_kernel, devices, groups),
         held,
@@ -401,7 +440,7 @@
         grid=(steps,),
         in_specs=[
             pl.BlockSpec(memory_space=pltpu.SMEM),
-            pl.BlockSpec((devices, block, 2 * LANES), lambda i: (0, part * steps + i, 0)),
+            pl.BlockSpec((devices, block, 2 * LANES), lambda i: (0, start + i, 0)),
             table,
             table,
         ],
@@ -439,74 +478,102 @@
 
 def inverse_kernel(first_block, per_device, zone_ref, table_ref, field_ref, *refs):
     cos_ref, sin_ref, mix_ref = refs[:3]
-    o_ref, token_ref, g_ref = refs[-3:]
+    o_ref, token_ref, f_ref, g_ref, e_ref = refs[-5:]
     token_ref[...] = jnp.zeros_like(token_ref)
     rows, width = o_ref.shape
     points = width // RADIX
-    block = first_block + pl.program_id(0)
-    field = field_ref[...].reshape(UNITS * rows, 2 * LANES)
-    g_ref[...] = jnp.dot(field, mix_ref[...], preferred_element_type=f32).reshape(
-        UNITS, rows, 4 * points
-    )
-
-    def tile(i, carry):
-        l = pl.multiple_of(i * LANES, LANES)
-
-        def load(residue):
-            if residue in (0, UNITS):
-                unit, second = 0, residue != 0
-            else:
-                unit, second = (residue, False) if residue < UNITS else (RADIX - residue, True)
-            unit = unit % GROUP * HALVES + unit // GROUP
-            start = 2 * points if second else 0
-            re = g_ref[unit, :, pl.ds(start + l, LANES)]
-            im = g_ref[unit, :, pl.ds(start + points + l, LANES)]
-            if residue == 0:
-                return (re, im)
-            c = cos_ref[residue : residue + 1, pl.ds(l, LANES)]
-            s = sin_ref[residue : residue + 1, pl.ds(l, LANES)]
-            return (re * c - im * s, im * c + re * s)
-
-        pixels = complex_fft([load(residue) for residue in range(RADIX)], 1)
-        for p in range(RADIX):
-            re, im = pixels[p]
-            power = jnp.maximum(re * re + im * im, DAMPING_FLOOR * DAMPING_FLOOR)
-            sine = im * lax.rsqrt(power)
-            zone = zone_ref[block * RADIX + p]
+    blocks = rows // ZB_R
+    block = first_block + pl.program_id(0) * blocks
+    lane = lax.broadcasted_iota(jnp.int32, (rows, 2 * LANES), 1)
+    first_residue = lane % LANES < LANES // 2
+
+    def unit(u):
+        return field_ref[u % GROUP, u // GROUP]
+
+    for k in range(UNITS):
+        f_ref[k] = jnp.where(first_residue, unit(k), unit(-k % UNITS))
+    g_ref[...] = jnp.dot(
+        f_ref[...].reshape(UNITS * rows, 2 * LANES), mix_ref[...], preferred_element_type=f32
+    ).reshape(UNITS, rows, 4 * points)
+
+    for p in range(RADIX):
+        for i in range(blocks):
+            zone = zone_ref[(block + i) * RADIX + p]
             base = zone // per_device * (4 * per_device) + zone % per_device
-            e = [table_ref[base + r * per_device] for r in range(4)]
-            height = e[0] + sine * (e[1] + sine * (e[2] + sine * e[3]))
-            o_ref[:, pl.ds(p * points + l, LANES)] = height.astype(bf16)
+            for r in range(4):
+                e_ref[i, r, p : p + 1, :] = jnp.full((1, LANES), table_ref[base + r * per_device], f32)
+
+    def tile(i, l):
+        here = pl.ds(i * ZB_R, ZB_R)
+        for odd in range(2):
+            def load(k):
+                start = odd * 2 * points
+                re = g_ref[k, here, pl.ds(start + l, LANES)]
+                im = g_ref[k, here, pl.ds(start + points + l, LANES)]
+                if k == 0:
+                    return (re, im)
+                row = odd * UNITS + k
+                c = cos_ref[row : row + 1, pl.ds(l, LANES)]
+                s = sin_ref[row : row + 1, pl.ds(l, LANES)]
+                return (re * c - im * s, im * c + re * s)
+
+            pixels = complex_fft([load(k) for k in range(UNITS)], 1)
+            for k in range(UNITS):
+                p = 2 * k + odd
+                re, im = pixels[k]
+                power = jnp.maximum(re * re + im * im, DAMPING_FLOOR * DAMPING_FLOOR)
+                sine = im * lax.rsqrt(power)
+                e = [e_ref[i, r, p : p + 1, :] for r in range(4)]
+                height = e[0] + sine * (e[1] + sine * (e[2] + sine * e[3]))
+                o_ref[here, pl.ds(p * points + l, LANES)] = height.astype(bf16)
+
+    def group(i, carry):
+        for t in range(points // LANES):
+            tile(i, t * LANES)
         return carry
 
-    lax.fori_loop(0, points // LANES, tile, 0)
+    if True:
+        lax.fori_loop(0, blocks, group, 0)
+    else:
+        def one(j, carry):
+            tile(j // (points // LANES), pl.multiple_of(j % (points // LANES) * LANES, LANES))
+            return carry
+        lax.fori_loop(0, blocks * (points // LANES), one, 0)
 
 
 def row_inverse(field, zones, table, previous, part, shape, per_device, *held):
     part_rows = field.shape[2]
     rows, width = shape
-    steps = part_rows // ZB_R
+    first = out_part(part, rows)[0]
+    block = min(16, part_rows)
+    steps = part_rows // block
+    start = first // block
     tables = inverse_tables(width)
     smem = pl.BlockSpec(memory_space=pltpu.SMEM)
     extra = [] if previous is None else [previous]
     operands = [zones, table, field, *[jnp.asarray(t) for t in tables], *extra]
     return launch(
-        functools.partial(inverse_kernel, part * steps, per_device),
+        functools.partial(inverse_kernel, first // ZB_R, per_device),
         held,
         operands,
         grid=(steps,),
         in_specs=[smem, smem]
-        + [pl.BlockSpec((GROUP, HALVES, ZB_R, 2 * LANES), lambda i: (0, 0, i, 0))]
+        + [pl.BlockSpec((GROUP, HALVES, block, 2 * LANES), lambda i: (0, 0, i, 0))]
         + [whole(t) for t in tables]
         + [pl.BlockSpec(memory_space=pl.ANY) for _ in extra],
         out_specs=[
-            pl.BlockSpec((ZB_R, width), lambda i: (part * steps + i, 0)),
+            pl.BlockSpec((block, width), lambda i: (start + i, 0)),
             pl.BlockSpec((8, LANES), lambda i: (0, 0)),
         ],
         out_shape=[jax.ShapeDtypeStruct(shape, bf16), jax.ShapeDtypeStruct((8, LANES), f32)],
-        scratch_shapes=[pltpu.VMEM((UNITS, ZB_R, 4 * width // RADIX), f32)],
+        scratch_shapes=[
+            pltpu.VMEM((UNITS, block, 2 * LANES), bf16),
+            pltpu.VMEM((UNITS, block, 4 * width // RADIX), f32),
+            pltpu.VMEM((block // ZB_R, 4, RADIX, LANES), f32),
+        ],
         aliases={len(operands) - 1: 0} if extra else {},
         name="row_inverse",
+        cost=10**12,
     )
 
 
@@ -531,7 +598,8 @@
 
     per_device = zone_table.shape[1]
     spread = jnp.broadcast_to(zone_table[None], (devices, 4, per_device))
-    table = lax.all_to_all(spread, every, split_axis=0, concat_axis=0, tiled=True).reshape(-1)
+    spread = lax.all_to_all(spread, every, split_axis=0, concat_axis=0, tiled=True)
+    table = spread.reshape(-1)
     zones = zone_index.reshape(-1)
 
     first_offset = 4 * group * rows
@@ -549,17 +617,19 @@
     lobes, late, arrived = [], [], []
     for part in part_list:
         held = [lobes[-1]] if part >= 1 else []
+        if part == 1:
+            held.append(spread)
         if part >= 2:
             held.append(arrived[part - 2])
         lobe, *late = row_forward(fringes, part, late, *held)
         lobes.append(lobe)
         arrived.append(exchange(lobe))
-    arrived_late = exchange(late[0])
     firsts = [[], []]
     last = lobes[-1]
     for part in part_list:
         last = column_first(arrived[part], *forward_phase, part, devices, last)
         firsts[0].append(last)
+    arrived_late = exchange(gate(late[0], firsts[0][-2]))
     terms = [column_middle(firsts[0], masks[0])]
 
     def send(pieces):
@@ -569,41 +639,42 @@
         ]
 
     shares = []
-
-    def finish(index, before):
-        h, part = index // ROW_PARTS, index % ROW_PARTS
-        held = [before] + (shares[index - 2][1:] if index >= 2 else [])
+    outs = len(OUT_PARTS)
+
+    def finish(index, before, *done):
+        h, part = index // outs, index % outs
+        held = [before] + [piece for i in done for piece in shares[i][1:]]
         pieces = column_last(terms[h], *inverse_phase, group.reshape(1), part, groups, *held)
         shares.append([pieces[0], *send(pieces)])
         return pieces[0]
 
-    last = terms[0]
-    for part in part_list:
-        last = finish(part, last)
-        if part % 2 == 1:
-            for other in (part - 1, part):
-                last = column_first(arrived_late, *forward_phase, other, devices, last)
-                firsts[1].append(last)
+    last = finish(0, terms[0])
+    last = finish(1, last)
+    last = finish(2, last, 0)
+    last = finish(3, last, 1)
+    last = column_first(arrived_late, *forward_phase, 0, devices, last)
+    firsts[1].append(last)
     terms.append(column_middle(firsts[1], masks[1], last))
-    last = terms[1]
-    fields, result, token = [], None, None
-
-    def gather(part, before):
-        total = add([shares[part], shares[ROW_PARTS + part]], before)
+    last = finish(4, terms[1], 2)
+    last = finish(5, last, 3)
+    last = finish(6, last, 4)
+    last = finish(7, last, 5)
+
+    fields, result = [], None
+
+    def gather(part, before, *done):
+        total = add([shares[part], shares[outs + part]], before, *done)
         fields.append(exchange(total))
         return total
 
-    for part in part_list:
-        last = finish(ROW_PARTS + part, last)
-        if part >= 2:
-            last = gather(part - 2, last)
-    for part in part_list:
-        result, token = row_inverse(
+    for part in range(2):
+        last = gather(part, last)
+    for part in range(outs):
+        result, last = row_inverse(
             fields[part], zones, table, result, part, (rows // 2, width), per_device, last
         )
-        last = token
-        if part + 2 < ROW_PARTS:
-            last = gather(part + 2, last)
+        if part + 2 < outs:
+            last = gather(part + 2, last, fields[part + 1])
     return result
 
 

time: 779 us -> 723 us (0.928)
  waiting for transfers between devices: 155 us -> 256 us
  Pallas kernels: 483 us -> 384 us
  blocking collectives: 31.5 us -> 0 us
  starting transfers between devices: 82.8 us -> 61.1 us
    pallas_call x30 -> x28, Pallas kernels: 483 us -> 384 us  [launch(): pl.pallas_call(lambda *refs: kernel(*refs[count:]), in_specs=[pl.BlockSpe...]
    ppermute x8, waiting for transfers between devices: 117 us -> 204 us  [send(): lax.ppermute(pieces[d], 'group', [(g, (g + d) % groups) for g in range(gr...]
    all_to_all x1 -> x0, blocking collectives: 31.5 us -> none  [exchange(): lax.all_to_all(block, inside, split_axis=0, concat_axis=0, tiled=True)]
    all_to_all x1, starting transfers between devices: 23.7 us -> 7.3 us  [body(): lax.all_to_all(spread, every, split_axis=0, concat_axis=0, tiled=True)]
    all_to_all x8 -> x9, waiting for transfers between devices: 38.5 us -> 52.3 us  [exchange(): lax.all_to_all(block, inside, split_axis=0, concat_axis=0, tiled=True)]
    all_to_all x8 -> x9, starting transfers between devices: 47.4 us -> 41.4 us  [exchange(): lax.all_to_all(block, inside, split_axis=0, concat_axis=0, tiled=True)]
  transfers between devices with their start and end apart: 17 -> 18, of which waited for: 7 -> 12; matrix products, arithmetic and copies ran while one was open for 1% -> 1% of each run, Pallas kernels for 53% -> 47%
where the time goes in v2:
time: 723 us; the launch traced here: 721 us
  Pallas kernels  384 us (53%)
  waiting for transfers between devices  256 us (35%)
  starting transfers between devices  61.1 us (8%)
  local copies, waits for them, and re-layouts  14.4 us (2%)
    pallas_call x28, Pallas kernels, launch(): pl.pallas_call(lambda *refs: kernel(*refs[count:]), in_specs=[pl.BlockSpe...  384 us
    ppermute x8, waiting for transfers between devices, send(): lax.ppermute(pieces[d], 'group', [(g, (g + d) % groups) for g in range(gr...  204 us
    all_to_all x9, waiting for transfers between devices, exchange(): lax.all_to_all(block, inside, split_axis=0, concat_axis=0, tiled=True)  52.3 us
    all_to_all x9, starting transfers between devices, exchange(): lax.all_to_all(block, inside, split_axis=0, concat_axis=0, tiled=True)  41.4 us
  transfers between devices with their start and end apart: 18, of which 12 were waited for; matrix products, arithmetic and copies ran while one was open for 1% of the time, Pallas kernels for 47%

profile of v2, /device:TPU:0, one launch (start us, length us, event | category | flops | bytes accessed | tf_op | source)
XLA Modules:
  0.0 721.2 jit_solution(9931154339831543063)
XLA Ops:
  1.4 7.3 %all-to-all-start = ((f32[32,1,128]{2,1,0:T(1,128)}), f32[32,1,128]{2,1,0:T(1,128)S(1)}, u32[]{:S(2)}, u32[]{:S(2)}) async-start(f32[32,1,128]{2,1,0:T(1,128)} %reshape.174), calls=%async_computation | async-start | bytes 32768 | tf_op jit(solution)/shard_map/all_to_all | solution.py:601
  8.7 26.3 %row_forward.4 = (bf16[16,256,256]{2,1,0:T(8,128)(2,1)}, bf16[16,1024,256]{2,1,0:T(8,128)(2,1)}) custom-call(bf16[1024,32768]{1,0:T(8,128)(2,1)} %refs_2_.6, f32[33,512]{1,0:T(8,128)} %constant.108.clone.refs_1_.refs_3_, f32[33,512]{1,0:T(8,128)} %constant.109.clone.refs_2_.refs_4_, bf16[1024,256]{1,0:T(8,128)(2,1)} %constant.110.clone.refs_3_.refs_5_), custom_call_target="tpu_custom_call" | custom-call | flops 1 | bytes 1 | tf_op jit(solution)/shard_map/row_forward/pallas_call | solution.py:208
  41.9 26.5 %row_forward.5 = (bf16[16,256,256]{2,1,0:T(8,128)(2,1)}, bf16[16,1024,256]{2,1,0:T(8,128)(2,1)}) custom-call(bf16[16,256,256]{2,1,0:T(8,128)(2,1)} %get-tuple-element.36.refs_0_, f32[32,4,32]{2,1,0:T(4,128)} %reshape.175.refs_1_, bf16[1024,32768]{1,0:T(8,128)(2,1)} %refs_2_.6, ...), custom_call_target="tpu_custom_call", output_to_operand_aliasing={{1}: (6, {})} | custom-call | flops 1 | bytes 1 | tf_op jit(solution)/shard_map/row_forward/pallas_call | solution.py:208
  73.5 26.5 %row_forward.6 = (bf16[16,256,256]{2,1,0:T(8,128)(2,1)}, bf16[16,1024,256]{2,1,0:T(8,128)(2,1)}) custom-call(bf16[16,256,256]{2,1,0:T(8,128)(2,1)} %get-tuple-element.38.refs_0_, bf16[16,256,256]{2,1,0:T(8,128)(2,1)} %copy-done, bf16[1024,32768]{1,0:T(8,128)(2,1)} %refs_2_.6, ...), custom_call_target="tpu_custom_call", output_to_operand_aliasing={{1}: (6, {})} | custom-call | flops 1 | bytes 1 | tf_op jit(solution)/shard_map/row_forward/pallas_call | solution.py:208
  105.1 26.5 %row_forward.7 = (bf16[16,256,256]{2,1,0:T(8,128)(2,1)}, bf16[16,1024,256]{2,1,0:T(8,128)(2,1)}) custom-call(bf16[16,256,256]{2,1,0:T(8,128)(2,1)} %get-tuple-element.40.refs_0_, bf16[16,256,256]{2,1,0:T(8,128)(2,1)} %all-to-all-done.2.refs_1_, bf16[1024,32768]{1,0:T(8,128)(2,1)} %refs_2_.6, ...), custom_call_target="tpu_custom_call", output_to_operand_aliasing={{1}: (6, {})} | custom-call | flops 1 | bytes 1 | tf_op jit(solution)/shard_map/row_forward/pallas_call | solution.py:208
  141.4 6.6 column_first.5.refs_0_
  148.0 6.6 column_first.6.refs_0_.refs_1_
  154.6 6.6 column_first.7.refs_0_.refs_2_
  181.4 28.2 %column_middle.2.refs_0_.refs_2_.refs_3_ = bf16[32,512,256]{2,1,0:T(8,128)(2,1)} custom-call(bf16[32,256,256]{2,1,0:T(8,128)(2,1)} %column_first.5.refs_0_, bf16[32,256,256]{2,1,0:T(8,128)(2,1)} %column_first.6.refs_0_.refs_1_, bf16[32,256,256]{2,1,0:T(8,128)(2,1)} %column_first.7.refs_0_.refs_2_, bf16[32,256,256]{2,1,0:T(8,128)(2,1)} %column_first.8.refs_3_, ...), custom_call_target="tpu_custom_call" | custom-call | flops 1 | bytes 1 | tf_op jit(solution)/shard_map/column_middle/pallas_call | solution.py:208
  223.2 71.6 %collective-permute-done.refs_1_.refs_2_ = bf16[16,128,256]{2,1,0:T(8,128)(2,1)S(1)} collective-permute-done((bf16[16,128,256]{2,1,0:T(8,128)(2,1)}, bf16[16,128,256]{2,1,0:T(8,128)(2,1)S(1)}, u32[]{:S(2)}, u32[]{:S(2)}) %collective-permute-start) | collective-permute-done | bytes 1048608 | tf_op jit(solution)/shard_map/ppermute | solution.py:637
  304.5 12.9 %collective-permute-done.1.refs_1_.refs_2_ = bf16[16,128,256]{2,1,0:T(8,128)(2,1)S(1)} collective-permute-done((bf16[16,128,256]{2,1,0:T(8,128)(2,1)}, bf16[16,128,256]{2,1,0:T(8,128)(2,1)S(1)}, u32[]{:S(2)}, u32[]{:S(2)}) %collective-permute-start.1) | collective-permute-done | bytes 1048608 | tf_op jit(solution)/shard_map/ppermute | solution.py:637
  327.9 21.6 %column_first.9.refs_0_.refs_1_.refs_2_.refs_3_.refs_4_ = bf16[32,1024,256]{2,1,0:T(8,128)(2,1)} custom-call(bf16[16,128,256]{2,1,0:T(8,128)(2,1)} %get-tuple-element.48.refs_0_.refs_2_, bf16[16,1024,256]{2,1,0:T(8,128)(2,1)} %all-to-all-done.5.refs_1_, f32[1024,32]{1,0:T(8,128)} %get-tuple-element.68.refs_2_, f32[1024,32]{1,0:T(8,128)} %get-tuple-element.67.refs_3_), custom_call_target="tpu_custom_call" | custom-call | flops 1 | bytes 1 | tf_op jit(solution)/shard_map/column_first/pallas_call | solution.py:208
  349.5 28.2 %column_middle.3.refs_0_.refs_3_ = bf16[32,512,256]{2,1,0:T(8,128)(2,1)} custom-call(bf16[32,1024,256]{2,1,0:T(8,128)(2,1)} %column_first.9.refs_0_.refs_1_.refs_2_.refs_3_.refs_4_, bf16[32,1024,256]{2,1,0:T(8,128)(2,1)} %column_first.9.refs_0_.refs_1_.refs_2_.refs_3_.refs_4_, bf16[32,1024,256]{2,1,0:T(8,128)(2,1)} %column_first.9.refs_0_.refs_1_.refs_2_.refs_3_.refs_4_, ...), custom_call_target="tpu_custom_call" | custom-call | flops 1 | bytes 1 | tf_op jit(solution)/shard_map/column_middle/pallas_call | solution.py:208
  377.7 10.5 %collective-permute-done.2.refs_1_.refs_3_ = bf16[16,128,256]{2,1,0:T(8,128)(2,1)S(1)} collective-permute-done((bf16[16,128,256]{2,1,0:T(8,128)(2,1)}, bf16[16,128,256]{2,1,0:T(8,128)(2,1)S(1)}, u32[]{:S(2)}, u32[]{:S(2)}) %collective-permute-start.2) | collective-permute-done | bytes 1048608 | tf_op jit(solution)/shard_map/ppermute | solution.py:637
  394.5 38.6 %collective-permute-done.3.refs_1_.refs_3_ = bf16[16,128,256]{2,1,0:T(8,128)(2,1)S(1)} collective-permute-done((bf16[16,128,256]{2,1,0:T(8,128)(2,1)}, bf16[16,128,256]{2,1,0:T(8,128)(2,1)S(1)}, u32[]{:S(2)}, u32[]{:S(2)}) %collective-permute-start.3) | collective-permute-done | bytes 1048608 | tf_op jit(solution)/shard_map/ppermute | solution.py:637
  439.5 38.6 %collective-permute-done.4.refs_1_.refs_4_ = bf16[16,128,256]{2,1,0:T(8,128)(2,1)S(1)} collective-permute-done((bf16[16,128,256]{2,1,0:T(8,128)(2,1)}, bf16[16,128,256]{2,1,0:T(8,128)(2,1)S(1)}, u32[]{:S(2)}, u32[]{:S(2)}) %collective-permute-start.4) | collective-permute-done | bytes 1048608 | tf_op jit(solution)/shard_map/ppermute | solution.py:637
  484.5 16.0 %collective-permute-done.5.refs_1_.refs_4_ = bf16[16,128,256]{2,1,0:T(8,128)(2,1)S(1)} collective-permute-done((bf16[16,128,256]{2,1,0:T(8,128)(2,1)}, bf16[16,128,256]{2,1,0:T(8,128)(2,1)S(1)}, u32[]{:S(2)}, u32[]{:S(2)}) %collective-permute-start.5) | collective-permute-done | bytes 1048608 | tf_op jit(solution)/shard_map/ppermute | solution.py:637
  523.4 38.5 %all-to-all-done.6.refs_3_ = bf16[16,2,128,256]{3,2,1,0:T(8,128)(2,1)S(1)} async-done(((bf16[16,2,128,256]{3,2,1,0:T(8,128)(2,1)}), bf16[16,2,128,256]{3,2,1,0:T(8,128)(2,1)S(1)}, u32[]{:S(2)}, u32[]{:S(2)}) %all-to-all-start.6) | async-done | bytes 2097184 | tf_op jit(solution)/shard_map/all_to_all | solution.py:597
  566.6 28.3 %row_inverse.4 = (bf16[512,32768]{1,0:T(8,128)(2,1)}, f32[8,128]{1,0:T(8,128)}) custom-call(bf16[16,2,128,256]{3,2,1,0:T(8,128)(2,1)} %sum_shares.5.refs_0_, s32[2048]{0:T(1024)} %reshape.172.refs_1_, f32[4096]{0:T(1024)} %reshape.173.refs_2_, bf16[16,2,128,256]{3,2,1,0:T(8,128)(2,1)} %copy-done.9, f32[64,512]{1,0:T(8,128)} %constant.113.clone.refs_4_, ...), custom_call_target="tpu_custom_call" | custom-call | flops 999999995904 | bytes 999999995904 | tf_op jit(solution)/shard_map/row_inverse/pallas_call | solution.py:208
  594.9 15.5 %collective-permute-done.6.refs_5_ = bf16[16,128,256]{2,1,0:T(8,128)(2,1)} collective-permute-done((bf16[16,128,256]{2,1,0:T(8,128)(2,1)}, bf16[16,128,256]{2,1,0:T(8,128)(2,1)}, u32[]{:S(2)}, u32[]{:S(2)}) %collective-permute-start.6) | collective-permute-done | bytes 1048608 | tf_op jit(solution)/shard_map/ppermute | solution.py:637
  610.4 7.8 %all-to-all-done.7.refs_1_.refs_3_ = bf16[16,2,128,256]{3,2,1,0:T(8,128)(2,1)} async-done(((bf16[16,2,128,256]{3,2,1,0:T(8,128)(2,1)}), bf16[16,2,128,256]{3,2,1,0:T(8,128)(2,1)}, u32[]{:S(2)}, u32[]{:S(2)}) %all-to-all-start.7) | async-done | bytes 2097184 | tf_op jit(solution)/shard_map/all_to_all | solution.py:597
  627.0 28.3 %row_inverse.5 = (bf16[512,32768]{1,0:T(8,128)(2,1)}, f32[8,128]{1,0:T(8,128)}) custom-call(bf16[16,2,128,256]{3,2,1,0:T(8,128)(2,1)} %sum_shares.6.refs_0_, s32[2048]{0:T(1024)} %reshape.172.refs_1_, f32[4096]{0:T(1024)} %reshape.173.refs_2_, bf16[16,2,128,256]{3,2,1,0:T(8,128)(2,1)} %all-to-all-done.7.refs_1_.refs_3_, ...), custom_call_target="tpu_custom_call", output_to_operand_aliasing={{0}: (7, {})} | custom-call | flops 999999995904 | bytes 999999995904 | tf_op jit(solution)/shard_map/row_inverse/pallas_call | solution.py:208
  664.6 28.3 %row_inverse.6 = (bf16[512,32768]{1,0:T(8,128)(2,1)}, f32[8,128]{1,0:T(8,128)}) custom-call(bf16[16,2,128,256]{3,2,1,0:T(8,128)(2,1)} %sum_shares.7.refs_0_, s32[2048]{0:T(1024)} %reshape.172.refs_1_, f32[4096]{0:T(1024)} %reshape.173.refs_2_, bf16[16,2,128,256]{3,2,1,0:T(8,128)(2,1)} %all-to-all-done.8.refs_1_.refs_3_, ...), custom_call_target="tpu_custom_call", output_to_operand_aliasing={{0}: (7, {})} | custom-call | flops 999999995904 | bytes 999999995904 | tf_op jit(solution)/shard_map/row_inverse/pallas_call | solution.py:208
  692.9 28.3 %row_inverse.7 = (bf16[512,32768]{1,0:T(8,128)(2,1)}, f32[8,128]{1,0:T(8,128)}) custom-call(f32[8,128]{1,0:T(8,128)} %get-tuple-element.64.refs_0_, s32[2048]{0:T(1024)} %reshape.172.refs_1_, f32[4096]{0:T(1024)} %reshape.173.refs_2_, bf16[16,2,128,256]{3,2,1,0:T(8,128)(2,1)} %all-to-all-done.9.refs_3_, ...), custom_call_target="tpu_custom_call", output_to_operand_aliasing={{0}: (7, {})} | custom-call | flops 999999995904 | bytes 999999995904 | tf_op jit(solution)/shard_map/row_inverse/pallas_call | solution.py:208
  (88 shorter events, 146.8 us)
Async XLA Ops:
  1.4 33.7 %all-to-all-start = ((f32[32,1,128]{2,1,0:T(1,128)}), f32[32,1,128]{2,1,0:T(1,128)S(1)}, u32[]{:S(2)}, u32[]{:S(2)}) async-start(f32[32,1,128]{2,1,0:T(1,128)} %reshape.174), calls=%async_computation | async-start | bytes 32768 | tf_op jit(solution)/shard_map/all_to_all | solution.py:601
  35.1 33.3 %all-to-all-start.1 = ((bf16[16,256,256]{2,1,0:T(8,128)(2,1)}), bf16[16,256,256]{2,1,0:T(8,128)(2,1)S(1)}, u32[]{:S(2)}, u32[]{:S(2)}) async-start(bf16[16,256,256]{2,1,0:T(8,128)(2,1)} %get-tuple-element.36.refs_0_), calls=%async_computation.1 | async-start | bytes 4194304 | tf_op jit(solution)/shard_map/all_to_all | solution.py:597
  68.4 5.2 copy-start
  68.4 32.6 %all-to-all-start.2 = ((bf16[16,256,256]{2,1,0:T(8,128)(2,1)}), bf16[16,256,256]{2,1,0:T(8,128)(2,1)}, u32[]{:S(2)}, u32[]{:S(2)}) async-start(bf16[16,256,256]{2,1,0:T(8,128)(2,1)} %get-tuple-element.38.refs_0_), calls=%async_computation.2 | async-start | bytes 4194304 | tf_op jit(solution)/shard_map/all_to_all | solution.py:597
  100.9 31.5 %all-to-all-start.3 = ((bf16[16,256,256]{2,1,0:T(8,128)(2,1)}), bf16[16,256,256]{2,1,0:T(8,128)(2,1)S(1)}, u32[]{:S(2)}, u32[]{:S(2)}) async-start(bf16[16,256,256]{2,1,0:T(8,128)(2,1)} %get-tuple-element.40.refs_0_), calls=%async_computation.3 | async-start | bytes 4194304 | tf_op jit(solution)/shard_map/all_to_all | solution.py:597
  132.5 1.4 copy-start.2
  133.9 31.6 %all-to-all-start.4 = ((bf16[16,256,256]{2,1,0:T(8,128)(2,1)}), bf16[16,256,256]{2,1,0:T(8,128)(2,1)S(1)}, u32[]{:S(2)}, u32[]{:S(2)}) async-start(bf16[16,256,256]{2,1,0:T(8,128)(2,1)} %get-tuple-element.42.refs_0_), calls=%async_computation.4 | async-start | bytes 4194304 | tf_op jit(solution)/shard_map/all_to_all | solution.py:597
  161.2 10.5 %copy-start.12 = (s32[64,2]{0,1:T(2,128)S(1)}, s32[64,2]{0,1:T(2,128)}, u32[]{:S(2)}) copy-start(s32[64,2]{0,1:T(2,128)} %param.33) | copy-start | bytes 1540
  166.8 161.1 %all-to-all-start.5 = ((bf16[16,1024,256]{2,1,0:T(8,128)(2,1)}), bf16[16,1024,256]{2,1,0:T(8,128)(2,1)}, u32[]{:S(2)}, u32[]{:S(2)}) async-start(bf16[16,1024,256]{2,1,0:T(8,128)(2,1)} %gate.1), calls=%async_computation.5 | async-start | bytes 16777216 | tf_op jit(solution)/shard_map/all_to_all | solution.py:597
  214.9 79.9 %collective-permute-start = (bf16[16,128,256]{2,1,0:T(8,128)(2,1)}, bf16[16,128,256]{2,1,0:T(8,128)(2,1)S(1)}, u32[]{:S(2)}, u32[]{:S(2)}) collective-permute-start(bf16[16,128,256]{2,1,0:T(8,128)(2,1)} %get-tuple-element.45), channel_id=1, source_target_pairs={{0,4},{4,0},{1,5},{5,1},{2,6},{6,2},{3,7},{7,3},{8,12},{12,8},{9,1... | collective-permute-start | bytes 3145736 | tf_op jit(solution)/shard_map/ppermute | solution.py:637
  222.8 94.6 %collective-permute-start.1 = (bf16[16,128,256]{2,1,0:T(8,128)(2,1)}, bf16[16,128,256]{2,1,0:T(8,128)(2,1)S(1)}, u32[]{:S(2)}, u32[]{:S(2)}) collective-permute-start(bf16[16,128,256]{2,1,0:T(8,128)(2,1)} %get-tuple-element.47), channel_id=1, source_target_pairs={{0,4},{4,0},{1,5},{5,1},{2,6},{6,2},{3,7},{7,3},{8,12},{12,8},{9,1... | collective-permute-start | bytes 3145736 | tf_op jit(solution)/shard_map/ppermute | solution.py:637
  301.2 87.0 %collective-permute-start.2 = (bf16[16,128,256]{2,1,0:T(8,128)(2,1)}, bf16[16,128,256]{2,1,0:T(8,128)(2,1)S(1)}, u32[]{:S(2)}, u32[]{:S(2)}) collective-permute-start(bf16[16,128,256]{2,1,0:T(8,128)(2,1)} %get-tuple-element.50), channel_id=1, source_target_pairs={{0,4},{4,0},{1,5},{5,1},{2,6},{6,2},{3,7},{7,3},{8,12},{12,8},{9,1... | collective-permute-start | bytes 3145736 | tf_op jit(solution)/shard_map/ppermute | solution.py:637
  323.7 109.5 %collective-permute-start.3 = (bf16[16,128,256]{2,1,0:T(8,128)(2,1)}, bf16[16,128,256]{2,1,0:T(8,128)(2,1)S(1)}, u32[]{:S(2)}, u32[]{:S(2)}) collective-permute-start(bf16[16,128,256]{2,1,0:T(8,128)(2,1)} %get-tuple-element.52), channel_id=1, source_target_pairs={{0,4},{4,0},{1,5},{5,1},{2,6},{6,2},{3,7},{7,3},{8,12},{12,8},{9,1... | collective-permute-start | bytes 3145736 | tf_op jit(solution)/shard_map/ppermute | solution.py:637
  394.5 83.6 %collective-permute-start.4 = (bf16[16,128,256]{2,1,0:T(8,128)(2,1)}, bf16[16,128,256]{2,1,0:T(8,128)(2,1)S(1)}, u32[]{:S(2)}, u32[]{:S(2)}) collective-permute-start(bf16[16,128,256]{2,1,0:T(8,128)(2,1)} %get-tuple-element.54), channel_id=1, source_target_pairs={{0,4},{4,0},{1,5},{5,1},{2,6},{6,2},{3,7},{7,3},{8,12},{12,8},{9,1... | collective-permute-start | bytes 3145736 | tf_op jit(solution)/shard_map/ppermute | solution.py:637
  439.5 61.0 %collective-permute-start.5 = (bf16[16,128,256]{2,1,0:T(8,128)(2,1)}, bf16[16,128,256]{2,1,0:T(8,128)(2,1)S(1)}, u32[]{:S(2)}, u32[]{:S(2)}) collective-permute-start(bf16[16,128,256]{2,1,0:T(8,128)(2,1)} %get-tuple-element.56), channel_id=1, source_target_pairs={{0,4},{4,0},{1,5},{5,1},{2,6},{6,2},{3,7},{7,3},{8,12},{12,8},{9,1... | collective-permute-start | bytes 3145736 | tf_op jit(solution)/shard_map/ppermute | solution.py:637
  506.8 8.1 %copy-start.11 = (s32[32,64]{1,0:T(8,128)S(1)}, s32[32,64]{1,0:T(8,128)}, u32[]{:S(2)}) copy-start(s32[32,64]{1,0:T(8,128)} %param.34) | copy-start | bytes 24580
  506.8 8.7 %copy-start.10 = (f32[32,4,32]{2,1,0:T(4,128)S(1)}, f32[32,4,32]{2,1,0:T(4,128)}, u32[]{:S(2)}) copy-start(f32[32,4,32]{2,1,0:T(4,128)} %reshape.175.refs_1_) | copy-start | bytes 49156
  511.1 50.8 %all-to-all-start.6 = ((bf16[16,2,128,256]{3,2,1,0:T(8,128)(2,1)}), bf16[16,2,128,256]{3,2,1,0:T(8,128)(2,1)S(1)}, u32[]{:S(2)}, u32[]{:S(2)}) async-start(bf16[16,2,128,256]{3,2,1,0:T(8,128)(2,1)} %sum_shares.4.refs_0_), calls=%async_computation.6 | async-start | bytes 4194304 | tf_op jit(solution)/shard_map/all_to_all | solution.py:597
  516.2 139.0 %collective-permute-start.7 = (bf16[16,128,256]{2,1,0:T(8,128)(2,1)}, bf16[16,128,256]{2,1,0:T(8,128)(2,1)}, u32[]{:S(2)}, u32[]{:S(2)}) collective-permute-start(bf16[16,128,256]{2,1,0:T(8,128)(2,1)} %get-tuple-element.62), channel_id=1, source_target_pairs={{0,4},{4,0},{1,5},{5,1},{2,6},{6,2},{3,7},{7,3},{8,12},{12,8},{9,1... | collective-permute-start | bytes 3145736 | tf_op jit(solution)/shard_map/ppermute | solution.py:637
  516.2 94.1 %collective-permute-start.6 = (bf16[16,128,256]{2,1,0:T(8,128)(2,1)}, bf16[16,128,256]{2,1,0:T(8,128)(2,1)}, u32[]{:S(2)}, u32[]{:S(2)}) collective-permute-start(bf16[16,128,256]{2,1,0:T(8,128)(2,1)} %get-tuple-element.59), channel_id=1, source_target_pairs={{0,4},{4,0},{1,5},{5,1},{2,6},{6,2},{3,7},{7,3},{8,12},{12,8},{9,1... | collective-permute-start | bytes 3145736 | tf_op jit(solution)/shard_map/ppermute | solution.py:637
  561.9 4.7 copy-start.9
  561.9 56.3 %all-to-all-start.7 = ((bf16[16,2,128,256]{3,2,1,0:T(8,128)(2,1)}), bf16[16,2,128,256]{3,2,1,0:T(8,128)(2,1)}, u32[]{:S(2)}, u32[]{:S(2)}) async-start(bf16[16,2,128,256]{3,2,1,0:T(8,128)(2,1)} %sum_shares.5.refs_0_), calls=%async_computation.7 | async-start | bytes 4194304 | tf_op jit(solution)/shard_map/all_to_all | solution.py:597
  622.5 32.7 %all-to-all-start.8 = ((bf16[16,2,128,256]{3,2,1,0:T(8,128)(2,1)}), bf16[16,2,128,256]{3,2,1,0:T(8,128)(2,1)}, u32[]{:S(2)}, u32[]{:S(2)}) async-start(bf16[16,2,128,256]{3,2,1,0:T(8,128)(2,1)} %sum_shares.6.refs_0_), calls=%async_computation.8 | async-start | bytes 4194304 | tf_op jit(solution)/shard_map/all_to_all | solution.py:597
  659.6 33.4 %all-to-all-start.9 = ((bf16[16,2,128,256]{3,2,1,0:T(8,128)(2,1)}), bf16[16,2,128,256]{3,2,1,0:T(8,128)(2,1)}, u32[]{:S(2)}, u32[]{:S(2)}) async-start(bf16[16,2,128,256]{3,2,1,0:T(8,128)(2,1)} %sum_shares.7.refs_0_), calls=%async_computation.9 | async-start | bytes 4194304 | tf_op jit(solution)/shard_map/all_to_all | solution.py:597
  (7 other events, 7.2 us)

commit v3 on v2

--- a/solution.py
+++ b/solution.py
@@ -429,7 +429,7 @@
 def column_last(terms, cos_tab, sin_tab, group, part, groups, *held):
     devices, total, _ = terms.shape
     first, rows = out_part(part, total)
-    block = min(64, rows)
+    block = math.gcd(first, rows, 64)
     steps = rows // block
     start = first // block
     table = pl.BlockSpec((block, devices), lambda i: (start + i, 0))
@@ -460,7 +460,7 @@
         o_ref[:, h] = total.astype(bf16)
 
 
-def add(pieces, *held):
+def add(pieces, cost, *held):
     operands = [piece for shares in pieces for piece in shares]
     members, rows, lanes = operands[0].shape
     block = 4
@@ -473,6 +473,7 @@
         out_specs=pl.BlockSpec((block, HALVES, rows, lanes), lambda i: (i, 0, 0, 0)),
         out_shape=jax.ShapeDtypeStruct((members, HALVES, rows, lanes), bf16),
         name="sum_shares",
+        cost=cost,
     )
 
 
@@ -532,13 +533,7 @@
             tile(i, t * LANES)
         return carry
 
-    if True:
-        lax.fori_loop(0, blocks, group, 0)
-    else:
-        def one(j, carry):
-            tile(j // (points // LANES), pl.multiple_of(j % (points // LANES) * LANES, LANES))
-            return carry
-        lax.fori_loop(0, blocks * (points // LANES), one, 0)
+    lax.fori_loop(0, blocks, group, 0)
 
 
 def row_inverse(field, zones, table, previous, part, shape, per_device, *held):
@@ -657,18 +652,18 @@
     terms.append(column_middle(firsts[1], masks[1], last))
     last = finish(4, terms[1], 2)
     last = finish(5, last, 3)
-    last = finish(6, last, 4)
-    last = finish(7, last, 5)
 
     fields, result = [], None
 
     def gather(part, before, *done):
-        total = add([shares[part], shares[outs + part]], before, *done)
+        total = add([shares[part], shares[outs + part]], 10**12 if part == 1 else 1, before, *done)
         fields.append(exchange(total))
         return total
 
-    for part in range(2):
-        last = gather(part, last)
+    last = finish(6, last, 4)
+    last = finish(7, last)
+    last = gather(0, last)
+    last = gather(1, last)
     for part in range(outs):
         result, last = row_inverse(
             fields[part], zones, table, result, part, (rows // 2, width), per_device, last

time: 723 us -> 707 us (0.978)
  waiting for transfers between devices: 256 us -> 238 us
    ppermute x8, waiting for transfers between devices: 204 us -> 184 us  [send(): lax.ppermute(pieces[d], 'group', [(g, (g + d) % groups) for g in range(gr...]
  transfers between devices with their start and end apart: 18 -> 18, of which waited for: 12 -> 11; matrix products, arithmetic and copies ran while one was open for 1% -> 1% of each run, Pallas kernels for 47% -> 50%
where the time goes in v3:
time: 707 us; the launch traced here: 705 us
  Pallas kernels  384 us (54%)
  waiting for transfers between devices  238 us (34%)
  starting transfers between devices  61.9 us (9%)
  local copies, waits for them, and re-layouts  14.5 us (2%)
    pallas_call x28, Pallas kernels, launch(): pl.pallas_call(lambda *refs: kernel(*refs[count:]), in_specs=[pl.BlockSpe...  384 us
    ppermute x8, waiting for transfers between devices, send(): lax.ppermute(pieces[d], 'group', [(g, (g + d) % groups) for g in range(gr...  184 us
    all_to_all x9, waiting for transfers between devices, exchange(): lax.all_to_all(block, inside, split_axis=0, concat_axis=0, tiled=True)  54.1 us
    all_to_all x9, starting transfers between devices, exchange(): lax.all_to_all(block, inside, split_axis=0, concat_axis=0, tiled=True)  42.1 us
  transfers between devices with their start and end apart: 18, of which 11 were waited for; matrix products, arithmetic and copies ran while one was open for 1% of the time, Pallas kernels for 50%

profile of v3, /device:TPU:0, one launch (start us, length us, event | category | flops | bytes accessed | tf_op | source)
XLA Modules:
  0.0 704.7 jit_solution(11106611495092150508)
XLA Ops:
  1.4 7.3 %all-to-all-start = ((f32[32,1,128]{2,1,0:T(1,128)}), f32[32,1,128]{2,1,0:T(1,128)S(1)}, u32[]{:S(2)}, u32[]{:S(2)}) async-start(f32[32,1,128]{2,1,0:T(1,128)} %reshape.174), calls=%async_computation | async-start | bytes 32768 | tf_op jit(solution)/shard_map/all_to_all | solution.py:596
  8.7 26.3 %row_forward.4 = (bf16[16,256,256]{2,1,0:T(8,128)(2,1)}, bf16[16,1024,256]{2,1,0:T(8,128)(2,1)}) custom-call(bf16[1024,32768]{1,0:T(8,128)(2,1)} %refs_2_.6, f32[33,512]{1,0:T(8,128)} %constant.108.clone.refs_1_.refs_3_, f32[33,512]{1,0:T(8,128)} %constant.109.clone.refs_2_.refs_4_, bf16[1024,256]{1,0:T(8,128)(2,1)} %constant.110.clone.refs_3_.refs_5_), custom_call_target="tpu_custom_call" | custom-call | flops 1 | bytes 1 | tf_op jit(solution)/shard_map/row_forward/pallas_call | solution.py:208
  42.1 26.5 %row_forward.5 = (bf16[16,256,256]{2,1,0:T(8,128)(2,1)}, bf16[16,1024,256]{2,1,0:T(8,128)(2,1)}) custom-call(bf16[16,256,256]{2,1,0:T(8,128)(2,1)} %get-tuple-element.36.refs_0_, f32[32,4,32]{2,1,0:T(4,128)} %reshape.175.refs_1_, bf16[1024,32768]{1,0:T(8,128)(2,1)} %refs_2_.6, ...), custom_call_target="tpu_custom_call", output_to_operand_aliasing={{1}: (6, {})} | custom-call | flops 1 | bytes 1 | tf_op jit(solution)/shard_map/row_forward/pallas_call | solution.py:208
  73.8 26.5 %row_forward.6 = (bf16[16,256,256]{2,1,0:T(8,128)(2,1)}, bf16[16,1024,256]{2,1,0:T(8,128)(2,1)}) custom-call(bf16[16,256,256]{2,1,0:T(8,128)(2,1)} %get-tuple-element.38.refs_0_, bf16[16,256,256]{2,1,0:T(8,128)(2,1)} %copy-done, bf16[1024,32768]{1,0:T(8,128)(2,1)} %refs_2_.6, ...), custom_call_target="tpu_custom_call", output_to_operand_aliasing={{1}: (6, {})} | custom-call | flops 1 | bytes 1 | tf_op jit(solution)/shard_map/row_forward/pallas_call | solution.py:208
  105.3 26.5 %row_forward.7 = (bf16[16,256,256]{2,1,0:T(8,128)(2,1)}, bf16[16,1024,256]{2,1,0:T(8,128)(2,1)}) custom-call(bf16[16,256,256]{2,1,0:T(8,128)(2,1)} %get-tuple-element.40.refs_0_, bf16[16,256,256]{2,1,0:T(8,128)(2,1)} %all-to-all-done.2.refs_1_, bf16[1024,32768]{1,0:T(8,128)(2,1)} %refs_2_.6, ...), custom_call_target="tpu_custom_call", output_to_operand_aliasing={{1}: (6, {})} | custom-call | flops 1 | bytes 1 | tf_op jit(solution)/shard_map/row_forward/pallas_call | solution.py:208
  141.6 6.6 column_first.5.refs_0_
  148.3 6.7 column_first.6.refs_0_.refs_1_
  154.9 6.7 column_first.7.refs_0_.refs_2_
  175.0 6.7 column_first.8.refs_3_
  181.7 28.2 %column_middle.2.refs_0_.refs_2_.refs_3_ = bf16[32,512,256]{2,1,0:T(8,128)(2,1)} custom-call(bf16[32,256,256]{2,1,0:T(8,128)(2,1)} %column_first.5.refs_0_, bf16[32,256,256]{2,1,0:T(8,128)(2,1)} %column_first.6.refs_0_.refs_1_, bf16[32,256,256]{2,1,0:T(8,128)(2,1)} %column_first.7.refs_0_.refs_2_, bf16[32,256,256]{2,1,0:T(8,128)(2,1)} %column_first.8.refs_3_, ...), custom_call_target="tpu_custom_call" | custom-call | flops 1 | bytes 1 | tf_op jit(solution)/shard_map/column_middle/pallas_call | solution.py:208
  223.7 71.4 %collective-permute-done.refs_1_.refs_2_ = bf16[16,128,256]{2,1,0:T(8,128)(2,1)S(1)} collective-permute-done((bf16[16,128,256]{2,1,0:T(8,128)(2,1)}, bf16[16,128,256]{2,1,0:T(8,128)(2,1)S(1)}, u32[]{:S(2)}, u32[]{:S(2)}) %collective-permute-start) | collective-permute-done | bytes 1048608 | tf_op jit(solution)/shard_map/ppermute | solution.py:632
  304.7 12.8 %collective-permute-done.1.refs_1_.refs_2_ = bf16[16,128,256]{2,1,0:T(8,128)(2,1)S(1)} collective-permute-done((bf16[16,128,256]{2,1,0:T(8,128)(2,1)}, bf16[16,128,256]{2,1,0:T(8,128)(2,1)S(1)}, u32[]{:S(2)}, u32[]{:S(2)}) %collective-permute-start.1) | collective-permute-done | bytes 1048608 | tf_op jit(solution)/shard_map/ppermute | solution.py:632
  328.2 21.6 %column_first.9.refs_0_.refs_1_.refs_2_.refs_3_.refs_4_ = bf16[32,1024,256]{2,1,0:T(8,128)(2,1)} custom-call(bf16[16,128,256]{2,1,0:T(8,128)(2,1)} %get-tuple-element.48.refs_0_.refs_2_, bf16[16,1024,256]{2,1,0:T(8,128)(2,1)} %all-to-all-done.5.refs_1_, f32[1024,32]{1,0:T(8,128)} %get-tuple-element.68.refs_2_, f32[1024,32]{1,0:T(8,128)} %get-tuple-element.67.refs_3_), custom_call_target="tpu_custom_call" | custom-call | flops 1 | bytes 1 | tf_op jit(solution)/shard_map/column_first/pallas_call | solution.py:208
  349.8 28.2 %column_middle.3.refs_0_.refs_3_.refs_2_ = bf16[32,512,256]{2,1,0:T(8,128)(2,1)} custom-call(bf16[32,1024,256]{2,1,0:T(8,128)(2,1)} %column_first.9.refs_0_.refs_1_.refs_2_.refs_3_.refs_4_, bf16[32,1024,256]{2,1,0:T(8,128)(2,1)} %column_first.9.refs_0_.refs_1_.refs_2_.refs_3_.refs_4_, ...), custom_call_target="tpu_custom_call" | custom-call | flops 1 | bytes 1 | tf_op jit(solution)/shard_map/column_middle/pallas_call | solution.py:208
  378.0 10.5 %collective-permute-done.2.refs_1_.refs_3_ = bf16[16,128,256]{2,1,0:T(8,128)(2,1)S(1)} collective-permute-done((bf16[16,128,256]{2,1,0:T(8,128)(2,1)}, bf16[16,128,256]{2,1,0:T(8,128)(2,1)S(1)}, u32[]{:S(2)}, u32[]{:S(2)}) %collective-permute-start.2) | collective-permute-done | bytes 1048608 | tf_op jit(solution)/shard_map/ppermute | solution.py:632
  394.8 38.6 %collective-permute-done.3.refs_1_.refs_3_ = bf16[16,128,256]{2,1,0:T(8,128)(2,1)S(1)} collective-permute-done((bf16[16,128,256]{2,1,0:T(8,128)(2,1)}, bf16[16,128,256]{2,1,0:T(8,128)(2,1)S(1)}, u32[]{:S(2)}, u32[]{:S(2)}) %collective-permute-start.3) | collective-permute-done | bytes 1048608 | tf_op jit(solution)/shard_map/ppermute | solution.py:632
  441.2 37.1 %collective-permute-done.4.refs_1_.refs_4_ = bf16[16,128,256]{2,1,0:T(8,128)(2,1)S(1)} collective-permute-done((bf16[16,128,256]{2,1,0:T(8,128)(2,1)}, bf16[16,128,256]{2,1,0:T(8,128)(2,1)S(1)}, u32[]{:S(2)}, u32[]{:S(2)}) %collective-permute-start.4) | collective-permute-done | bytes 1048608 | tf_op jit(solution)/shard_map/ppermute | solution.py:632
  507.2 39.6 %all-to-all-done.6.refs_3_ = bf16[16,2,128,256]{3,2,1,0:T(8,128)(2,1)} async-done(((bf16[16,2,128,256]{3,2,1,0:T(8,128)(2,1)}), bf16[16,2,128,256]{3,2,1,0:T(8,128)(2,1)}, u32[]{:S(2)}, u32[]{:S(2)}) %all-to-all-start.6) | async-done | bytes 2097184 | tf_op jit(solution)/shard_map/all_to_all | solution.py:592
  551.4 28.3 %row_inverse.4 = (bf16[512,32768]{1,0:T(8,128)(2,1)}, f32[8,128]{1,0:T(8,128)}) custom-call(bf16[16,2,128,256]{3,2,1,0:T(8,128)(2,1)} %sum_shares.5.refs_0_, s32[2048]{0:T(1024)} %reshape.172.refs_1_, f32[4096]{0:T(1024)} %reshape.173.refs_2_, bf16[16,2,128,256]{3,2,1,0:T(8,128)(2,1)} %all-to-all-done.6.refs_3_, f32[64,512]{1,0:T(8,128)} %constant.113.clone.refs_4_, ...), custom_call_target="tpu_custom_call" | custom-call | flops 999999995904 | bytes 999999995904 | tf_op jit(solution)/shard_map/row_inverse/pallas_call | solution.py:208
  579.7 13.3 %collective-permute-done.6.refs_5_ = bf16[16,128,256]{2,1,0:T(8,128)(2,1)} collective-permute-done((bf16[16,128,256]{2,1,0:T(8,128)(2,1)}, bf16[16,128,256]{2,1,0:T(8,128)(2,1)}, u32[]{:S(2)}, u32[]{:S(2)}) %collective-permute-start.6) | collective-permute-done | bytes 1048608 | tf_op jit(solution)/shard_map/ppermute | solution.py:632
  593.0 8.7 %all-to-all-done.7.refs_1_.refs_3_ = bf16[16,2,128,256]{3,2,1,0:T(8,128)(2,1)} async-done(((bf16[16,2,128,256]{3,2,1,0:T(8,128)(2,1)}), bf16[16,2,128,256]{3,2,1,0:T(8,128)(2,1)}, u32[]{:S(2)}, u32[]{:S(2)}) %all-to-all-start.7) | async-done | bytes 2097184 | tf_op jit(solution)/shard_map/all_to_all | solution.py:592
  610.5 28.3 %row_inverse.5 = (bf16[512,32768]{1,0:T(8,128)(2,1)}, f32[8,128]{1,0:T(8,128)}) custom-call(bf16[16,2,128,256]{3,2,1,0:T(8,128)(2,1)} %sum_shares.6.refs_0_, s32[2048]{0:T(1024)} %reshape.172.refs_1_, f32[4096]{0:T(1024)} %reshape.173.refs_2_, bf16[16,2,128,256]{3,2,1,0:T(8,128)(2,1)} %all-to-all-done.7.refs_1_.refs_3_, ...), custom_call_target="tpu_custom_call", output_to_operand_aliasing={{0}: (7, {})} | custom-call | flops 999999995904 | bytes 999999995904 | tf_op jit(solution)/shard_map/row_inverse/pallas_call | solution.py:208
  648.2 28.2 %row_inverse.6 = (bf16[512,32768]{1,0:T(8,128)(2,1)}, f32[8,128]{1,0:T(8,128)}) custom-call(bf16[16,2,128,256]{3,2,1,0:T(8,128)(2,1)} %sum_shares.7.refs_0_, s32[2048]{0:T(1024)} %reshape.172.refs_1_, f32[4096]{0:T(1024)} %reshape.173.refs_2_, bf16[16,2,128,256]{3,2,1,0:T(8,128)(2,1)} %all-to-all-done.8.refs_1_.refs_3_, ...), custom_call_target="tpu_custom_call", output_to_operand_aliasing={{0}: (7, {})} | custom-call | flops 999999995904 | bytes 999999995904 | tf_op jit(solution)/shard_map/row_inverse/pallas_call | solution.py:208
  676.4 28.3 %row_inverse.7 = (bf16[512,32768]{1,0:T(8,128)(2,1)}, f32[8,128]{1,0:T(8,128)}) custom-call(f32[8,128]{1,0:T(8,128)} %get-tuple-element.64.refs_0_, s32[2048]{0:T(1024)} %reshape.172.refs_1_, f32[4096]{0:T(1024)} %reshape.173.refs_2_, bf16[16,2,128,256]{3,2,1,0:T(8,128)(2,1)} %all-to-all-done.9.refs_3_, ...), custom_call_target="tpu_custom_call", output_to_operand_aliasing={{0}: (7, {})} | custom-call | flops 999999995904 | bytes 999999995904 | tf_op jit(solution)/shard_map/row_inverse/pallas_call | solution.py:208
  (86 shorter events, 141.4 us)
Async XLA Ops:
  1.4 33.7 %all-to-all-start = ((f32[32,1,128]{2,1,0:T(1,128)}), f32[32,1,128]{2,1,0:T(1,128)S(1)}, u32[]{:S(2)}, u32[]{:S(2)}) async-start(f32[32,1,128]{2,1,0:T(1,128)} %reshape.174), calls=%async_computation | async-start | bytes 32768 | tf_op jit(solution)/shard_map/all_to_all | solution.py:596
  35.1 33.5 %all-to-all-start.1 = ((bf16[16,256,256]{2,1,0:T(8,128)(2,1)}), bf16[16,256,256]{2,1,0:T(8,128)(2,1)S(1)}, u32[]{:S(2)}, u32[]{:S(2)}) async-start(bf16[16,256,256]{2,1,0:T(8,128)(2,1)} %get-tuple-element.36.refs_0_), calls=%async_computation.1 | async-start | bytes 4194304 | tf_op jit(solution)/shard_map/all_to_all | solution.py:592
  68.6 5.2 copy-start
  68.6 32.6 %all-to-all-start.2 = ((bf16[16,256,256]{2,1,0:T(8,128)(2,1)}), bf16[16,256,256]{2,1,0:T(8,128)(2,1)}, u32[]{:S(2)}, u32[]{:S(2)}) async-start(bf16[16,256,256]{2,1,0:T(8,128)(2,1)} %get-tuple-element.38.refs_0_), calls=%async_computation.2 | async-start | bytes 4194304 | tf_op jit(solution)/shard_map/all_to_all | solution.py:592
  101.2 31.5 %all-to-all-start.3 = ((bf16[16,256,256]{2,1,0:T(8,128)(2,1)}), bf16[16,256,256]{2,1,0:T(8,128)(2,1)S(1)}, u32[]{:S(2)}, u32[]{:S(2)}) async-start(bf16[16,256,256]{2,1,0:T(8,128)(2,1)} %get-tuple-element.40.refs_0_), calls=%async_computation.3 | async-start | bytes 4194304 | tf_op jit(solution)/shard_map/all_to_all | solution.py:592
  132.7 1.4 copy-start.2
  134.1 31.6 %all-to-all-start.4 = ((bf16[16,256,256]{2,1,0:T(8,128)(2,1)}), bf16[16,256,256]{2,1,0:T(8,128)(2,1)S(1)}, u32[]{:S(2)}, u32[]{:S(2)}) async-start(bf16[16,256,256]{2,1,0:T(8,128)(2,1)} %get-tuple-element.42.refs_0_), calls=%async_computation.4 | async-start | bytes 4194304 | tf_op jit(solution)/shard_map/all_to_all | solution.py:592
  161.6 10.4 %copy-start.10 = (s32[64,2]{0,1:T(2,128)S(1)}, s32[64,2]{0,1:T(2,128)}, u32[]{:S(2)}) copy-start(s32[64,2]{0,1:T(2,128)} %param.33) | copy-start | bytes 1540
  165.7 1.3 copy-start.1
  167.0 161.2 %all-to-all-start.5 = ((bf16[16,1024,256]{2,1,0:T(8,128)(2,1)}), bf16[16,1024,256]{2,1,0:T(8,128)(2,1)}, u32[]{:S(2)}, u32[]{:S(2)}) async-start(bf16[16,1024,256]{2,1,0:T(8,128)(2,1)} %gate.1), calls=%async_computation.5 | async-start | bytes 16777216 | tf_op jit(solution)/shard_map/all_to_all | solution.py:592
  215.3 79.8 %collective-permute-start = (bf16[16,128,256]{2,1,0:T(8,128)(2,1)}, bf16[16,128,256]{2,1,0:T(8,128)(2,1)S(1)}, u32[]{:S(2)}, u32[]{:S(2)}) collective-permute-start(bf16[16,128,256]{2,1,0:T(8,128)(2,1)} %get-tuple-element.45), channel_id=1, source_target_pairs={{0,4},{4,0},{1,5},{5,1},{2,6},{6,2},{3,7},{7,3},{8,12},{12,8},{9,1... | collective-permute-start | bytes 3145736 | tf_op jit(solution)/shard_map/ppermute | solution.py:632
  223.2 94.3 %collective-permute-start.1 = (bf16[16,128,256]{2,1,0:T(8,128)(2,1)}, bf16[16,128,256]{2,1,0:T(8,128)(2,1)S(1)}, u32[]{:S(2)}, u32[]{:S(2)}) collective-permute-start(bf16[16,128,256]{2,1,0:T(8,128)(2,1)} %get-tuple-element.47), channel_id=1, source_target_pairs={{0,4},{4,0},{1,5},{5,1},{2,6},{6,2},{3,7},{7,3},{8,12},{12,8},{9,1... | collective-permute-start | bytes 3145736 | tf_op jit(solution)/shard_map/ppermute | solution.py:632
  301.5 87.0 %collective-permute-start.2 = (bf16[16,128,256]{2,1,0:T(8,128)(2,1)}, bf16[16,128,256]{2,1,0:T(8,128)(2,1)S(1)}, u32[]{:S(2)}, u32[]{:S(2)}) collective-permute-start(bf16[16,128,256]{2,1,0:T(8,128)(2,1)} %get-tuple-element.50), channel_id=1, source_target_pairs={{0,4},{4,0},{1,5},{5,1},{2,6},{6,2},{3,7},{7,3},{8,12},{12,8},{9,1... | collective-permute-start | bytes 3145736 | tf_op jit(solution)/shard_map/ppermute | solution.py:632
  323.9 109.4 %collective-permute-start.3 = (bf16[16,128,256]{2,1,0:T(8,128)(2,1)}, bf16[16,128,256]{2,1,0:T(8,128)(2,1)S(1)}, u32[]{:S(2)}, u32[]{:S(2)}) collective-permute-start(bf16[16,128,256]{2,1,0:T(8,128)(2,1)} %get-tuple-element.52), channel_id=1, source_target_pairs={{0,4},{4,0},{1,5},{5,1},{2,6},{6,2},{3,7},{7,3},{8,12},{12,8},{9,1... | collective-permute-start | bytes 3145736 | tf_op jit(solution)/shard_map/ppermute | solution.py:632
  394.7 83.6 %collective-permute-start.4 = (bf16[16,128,256]{2,1,0:T(8,128)(2,1)}, bf16[16,128,256]{2,1,0:T(8,128)(2,1)S(1)}, u32[]{:S(2)}, u32[]{:S(2)}) collective-permute-start(bf16[16,128,256]{2,1,0:T(8,128)(2,1)} %get-tuple-element.54), channel_id=1, source_target_pairs={{0,4},{4,0},{1,5},{5,1},{2,6},{6,2},{3,7},{7,3},{8,12},{12,8},{9,1... | collective-permute-start | bytes 3145736 | tf_op jit(solution)/shard_map/ppermute | solution.py:632
  434.4 5.5 copy-start.9
  434.4 6.1 copy-start.8
  439.8 62.1 %collective-permute-start.5 = (bf16[16,128,256]{2,1,0:T(8,128)(2,1)}, bf16[16,128,256]{2,1,0:T(8,128)(2,1)S(1)}, u32[]{:S(2)}, u32[]{:S(2)}) collective-permute-start(bf16[16,128,256]{2,1,0:T(8,128)(2,1)} %get-tuple-element.57), channel_id=1, source_target_pairs={{0,4},{4,0},{1,5},{5,1},{2,6},{6,2},{3,7},{7,3},{8,12},{12,8},{9,1... | collective-permute-start | bytes 3145736 | tf_op jit(solution)/shard_map/ppermute | solution.py:632
  494.5 52.3 %all-to-all-start.6 = ((bf16[16,2,128,256]{3,2,1,0:T(8,128)(2,1)}), bf16[16,2,128,256]{3,2,1,0:T(8,128)(2,1)}, u32[]{:S(2)}, u32[]{:S(2)}) async-start(bf16[16,2,128,256]{3,2,1,0:T(8,128)(2,1)} %sum_shares.4.refs_0_), calls=%async_computation.6 | async-start | bytes 4194304 | tf_op jit(solution)/shard_map/all_to_all | solution.py:592
  498.9 139.9 %collective-permute-start.7 = (bf16[16,128,256]{2,1,0:T(8,128)(2,1)}, bf16[16,128,256]{2,1,0:T(8,128)(2,1)}, u32[]{:S(2)}, u32[]{:S(2)}) collective-permute-start(bf16[16,128,256]{2,1,0:T(8,128)(2,1)} %get-tuple-element.62), channel_id=1, source_target_pairs={{0,4},{4,0},{1,5},{5,1},{2,6},{6,2},{3,7},{7,3},{8,12},{12,8},{9,1... | collective-permute-start | bytes 3145736 | tf_op jit(solution)/shard_map/ppermute | solution.py:632
  499.0 94.0 %collective-permute-start.6 = (bf16[16,128,256]{2,1,0:T(8,128)(2,1)}, bf16[16,128,256]{2,1,0:T(8,128)(2,1)}, u32[]{:S(2)}, u32[]{:S(2)}) collective-permute-start(bf16[16,128,256]{2,1,0:T(8,128)(2,1)} %get-tuple-element.59), channel_id=1, source_target_pairs={{0,4},{4,0},{1,5},{5,1},{2,6},{6,2},{3,7},{7,3},{8,12},{12,8},{9,1... | collective-permute-start | bytes 3145736 | tf_op jit(solution)/shard_map/ppermute | solution.py:632
  546.8 55.0 %all-to-all-start.7 = ((bf16[16,2,128,256]{3,2,1,0:T(8,128)(2,1)}), bf16[16,2,128,256]{3,2,1,0:T(8,128)(2,1)}, u32[]{:S(2)}, u32[]{:S(2)}) async-start(bf16[16,2,128,256]{3,2,1,0:T(8,128)(2,1)} %sum_shares.5.refs_0_), calls=%async_computation.7 | async-start | bytes 4194304 | tf_op jit(solution)/shard_map/all_to_all | solution.py:592
  606.0 32.8 %all-to-all-start.8 = ((bf16[16,2,128,256]{3,2,1,0:T(8,128)(2,1)}), bf16[16,2,128,256]{3,2,1,0:T(8,128)(2,1)}, u32[]{:S(2)}, u32[]{:S(2)}) async-start(bf16[16,2,128,256]{3,2,1,0:T(8,128)(2,1)} %sum_shares.6.refs_0_), calls=%async_computation.8 | async-start | bytes 4194304 | tf_op jit(solution)/shard_map/all_to_all | solution.py:592
  643.1 33.3 %all-to-all-start.9 = ((bf16[16,2,128,256]{3,2,1,0:T(8,128)(2,1)}), bf16[16,2,128,256]{3,2,1,0:T(8,128)(2,1)}, u32[]{:S(2)}, u32[]{:S(2)}) async-start(bf16[16,2,128,256]{3,2,1,0:T(8,128)(2,1)} %sum_shares.7.refs_0_), calls=%async_computation.9 | async-start | bytes 4194304 | tf_op jit(solution)/shard_map/all_to_all | solution.py:592
  (6 other events, 5.9 us)
